TPU v7x, 32 devices: a whole 2x2x4 slice. The times are simulated.
32 devices in a mesh: ens: 2 (over y), slab: 16 (over z, x, core).
Axes of the slice: x: 2, y: 2, z: 4, core: 2. Of those that a mesh axis runs over, the one named last changes fastest.
Arguments:
- starting_joint_sensitivities: float32 [8, 2, 128, 65536], P('ens', None, 'slab'), parts along dimension 0, may hold values from -6 to 6
- former_section_velocity: float32 [8, 2, 128, 65536], P('ens', None, 'slab'), parts along dimension 0, may hold values from -6 to 6
- nominal_coefficient_factors: float32 [14], P('ens'), parts along dimension 0, may hold values from 0.5 to 2
- unlocking_coefficients_by_grade: float32 [32], P('ens'), parts along dimension 0, may hold values from 0.2 to 5
- repression_grade_by_abundance: int32 [1024], replicated, may hold values from 0 to 15
- measured_outbreak_frequencies: int32 [128], replicated, may hold values from 1 to 99
- upper_bounds_per_abundance: int32 [128], P('slab'), may hold values from 32 to 64
Outputs:
- section_slope: float32 [8, 2, 128, 65536], P('ens', None, 'slab'), parts along dimension 0
There are 2 independent parts, one for each index of `ens`. A program takes and returns all parts, laid end to end along the dimension named above; an argument that names none is the same for every part. Nothing has to cross between parts.
All inputs are finite; a program needn't handle non-finite values.
Results may differ from a plain program's by a relative error of at most 0.00005.
Values sent between devices are 32-bit elements; how exact they have to be, the bound alone decides.
A program may use at most 576 MiB of HBM per device.

v0:
```python
import jax
import jax.numpy as jnp
from jax import lax
from jax.sharding import PartitionSpec as P

P2 = 1024


nominal_coefficient_basis = (2.0, 0.02, 1.0, 0.01, 0.02, 0.03, 0.002)
section_step = 0.125


def shifted(value, axis, steps):
    count = lax.axis_size(axis)
    first, last = (max(0, -steps), min(count, count - steps))
    return lax.ppermute(value, axis, [(source, source + steps) for source in range(first, last)])


def episode_share_stencil(measured_outbreak_frequencies, stencil_breadth):
    episode_extents = jnp.arange(stencil_breadth, dtype=jnp.int32)
    episode_shares = measured_outbreak_frequencies.astype(jnp.float32) * (
        episode_extents >= 1
    ).astype(jnp.float32)
    episode_shares = episode_shares / jnp.sum(episode_shares)
    backward_difference = episode_extents[:, None] - episode_extents[None, :]
    single_selector = (backward_difference[:, :, None] == episode_extents[None, None, :]).astype(
        jnp.float32
    )
    return jnp.dot(single_selector, episode_shares, precision=lax.Precision.HIGHEST)


def kon_rates(unlocking_coefficients_by_grade, repression_grade_by_abundance):
    levels = jnp.arange(unlocking_coefficients_by_grade.shape[0], dtype=jnp.int32)
    single_selector = (repression_grade_by_abundance[:, None] == levels[None, :]).astype(
        jnp.float32
    )
    return jnp.dot(
        single_selector, unlocking_coefficients_by_grade, precision=lax.Precision.HIGHEST
    )


def decay_term(field, upper_rows, m_count, coefficient_sequence_values):
    m_grid = m_count[None, None, :, None]
    return coefficient_sequence_values[3] * ((m_grid + 1.0) * upper_rows - m_grid * field)


def lattice_rates(field, mterm, inflow, m_count, coefficient_sequence_values, switch_rates, inside):
    (
        episode_jump,
        peptide_rate,
        silencing_rate,
        unused_rate,
        first_removal,
        partner_making,
        partner_removal,
    ) = [coefficient_sequence_values[position] for position in range(7)]
    comps, genes, rows, firsts, seconds = field.shape
    keep_three = ((0, 0), (0, 0), (0, 0))
    lower_a = jnp.pad(field[:, :, :, :-1, :], keep_three + ((1, 0), (0, 0)))
    upper_a = jnp.pad(field[:, :, :, 1:, :], keep_three + ((0, 1), (0, 0)))
    lower_c = jnp.pad(field[:, :, :, :, :-1], keep_three + ((0, 0), (1, 0)))
    upper_c = jnp.pad(field[:, :, :, :, 1:], keep_three + ((0, 0), (0, 1)))
    a_grid = jnp.arange(firsts, dtype=jnp.float32)[None, None, None, :, None]
    c_grid = jnp.arange(seconds, dtype=jnp.float32)[None, None, None, None, :]
    m_grid = m_count[None, None, :, None, None]
    kon_grid = switch_rates[None, None, None, None, :]
    gene_sign = jnp.array([1.0, -1.0], dtype=jnp.float32)[None, :, None, None, None]
    gene_on = jnp.array([0.0, 1.0], dtype=jnp.float32)[None, :, None, None, None]
    silent = field[:, 0:1]
    expressing = field[:, 1:2]
    total = mterm
    total = total + peptide_rate * m_grid * (lower_a - field)
    total = total + first_removal * ((a_grid + 1.0) * upper_a - a_grid * field)
    total = total + partner_making * a_grid * (lower_c - field)
    total = total + partner_removal * ((c_grid + 1.0) * upper_c - c_grid * field)
    total = (
        total
        + gene_sign * (silencing_rate * expressing - kon_grid * silent)
        + gene_on * (episode_jump * (inflow - expressing))
    )
    component_index = jnp.arange(comps, dtype=jnp.int32)[:, None, None, None, None]
    first_pick = (component_index == 1).astype(jnp.float32)
    second_pick = (component_index == 2).astype(jnp.float32)
    third_pick = (component_index == 3).astype(jnp.float32)
    probability = field[0:1]
    probability_on = probability[:, 1:2]
    sources = first_pick * (gene_on * (episode_jump * (inflow[0:1] - probability_on)))
    sources = sources + second_pick * (peptide_rate * m_grid * (lower_a[0:1] - probability))
    sources = sources + third_pick * (gene_sign * (silencing_rate * probability_on))
    return inside * (total + sources)


def local(
    starting_joint_sensitivities,
    former_section_velocity,
    nominal_coefficient_factors,
    unlocking_coefficients_by_grade,
    repression_grade_by_abundance,
    measured_outbreak_frequencies,
    upper_bounds_per_abundance,
):
    comps, genes, rows, cell_total = starting_joint_sensitivities.shape
    firsts = cell_total // P2
    coefficient_sequence_values = nominal_coefficient_factors * jnp.array(
        nominal_coefficient_basis, dtype=jnp.float32
    )
    flat_index = jnp.arange(cell_total, dtype=jnp.int32)
    first_index = flat_index // P2
    inside = (first_index[None, :] < upper_bounds_per_abundance[:, None]).astype(jnp.float32)
    inside = inside[None, None, :, :]
    solution_tensor = inside * (
        starting_joint_sensitivities + section_step * former_section_velocity
    )
    stencil_breadth = measured_outbreak_frequencies.shape[0]
    episode_convolution = episode_share_stencil(measured_outbreak_frequencies, stencil_breadth)
    switch_rates = kon_rates(unlocking_coefficients_by_grade, repression_grade_by_abundance)
    first_row = lax.axis_index("slab") * rows
    m_count = (first_row + jnp.arange(rows, dtype=jnp.int32)).astype(jnp.float32)
    summed = jnp.einsum(
        "mn,cgnq->cgmq",
        episode_convolution,
        lax.all_to_all(solution_tensor[:, 1:2], "slab", split_axis=3, concat_axis=2, tiled=True),
        precision=lax.Precision.HIGHEST,
    )
    removal_inflow_term = lax.all_to_all(summed, "slab", split_axis=2, concat_axis=3, tiled=True)
    from_above = shifted(solution_tensor[:, :, 0:1], "slab", -1)
    upper_rows = jnp.concatenate([solution_tensor[:, :, 1:], from_above], axis=2)
    mterm = decay_term(solution_tensor, upper_rows, m_count, coefficient_sequence_values)
    field_view = solution_tensor.reshape(comps, genes, rows, firsts, P2)
    mterm_view = mterm.reshape(comps, genes, rows, firsts, P2)
    inflow_view = removal_inflow_term.reshape(comps, 1, rows, firsts, P2)
    inside_view = inside.reshape(1, 1, rows, firsts, P2)
    slope_view = lattice_rates(
        field_view,
        mterm_view,
        inflow_view,
        m_count,
        coefficient_sequence_values,
        switch_rates,
        inside_view,
    )
    return slope_view.reshape(comps, genes, rows, cell_total)


def solution(mesh):
    placed = (
        P("ens", None, "slab", None),
        P("ens", None, "slab", None),
        P("ens"),
        P("ens"),
        P(),
        P(),
        P("slab"),
    )
    return jax.shard_map(
        local, mesh=mesh, in_specs=placed, out_specs=P("ens", None, "slab", None), check_vma=False
    )
```

profile of v0, /device:TPU:11, one launch (start us, length us, event | category | flops | bytes accessed | tf_op | source)
XLA Modules:
  0.0 1234.9 jit_solution(2427363093807184793)
XLA Ops:
  0.9 11.4 add_multiply_fusion
  12.3 6.2 copy-done.2
  22.3 85.8 %copy.73 = f32[4,1,8,65536]{2,0,1,3:T(4,128)} copy(f32[4,1,8,65536]{3,2,1,0:T(8,128)} %slice.96) | data formatting | bytes 16777216 | tf_op jit(solution)/shard_map/slice | solution.py:122
  108.1 223.6 %reshape.162 = f32[16,1,131072]{2,1,0:T(1,128)} reshape(f32[65536,1,4,8]{3,2,1,0:T(4,128)} %bitcast.62) | data formatting | bytes 16777216
  331.7 7.1 all-to-all-start
  346.3 14.7 %slice.88 = f32[4,2,7,65536]{3,2,1,0:T(8,128)} slice(f32[4,2,8,65536]{3,2,1,0:T(8,128)} %copy-done.2), slice={[0:4], [0:2], [1:8], [0:65536]} | slice | bytes 29360128 | tf_op jit(solution)/shard_map/slice | solution.py:127
  361.0 4.4 copy.120
  365.4 11.8 fusion.35
  377.2 17.5 %copy.118 = f32[4,2,8,63,1024]{4,3,2,1,0:T(8,128)} copy(f32[4,2,8,63,1024]{4,2,3,1,0:T(8,128)} %get-tuple-element.7) | data formatting | bytes 33030144
  394.8 19.3 %fusion.36 = (f32[4,2,8,64,1023]{4,2,3,1,0:T(8,128)S(1)}, f32[4,2,8,64,1023]{4,2,3,1,0:T(8,128)}) fusion(f32[4,2,8,64,1024]{4,2,3,1,0:T(8,128)} %bitcast.67), kind=kLoop, calls=%fused_computation.70 | loop fusion | bytes 67043328 | tf_op jit(solution)/shard_map/slice | solution.py:61
  414.0 18.4 %copy.115 = f32[4,2,8,64,1023]{4,3,2,1,0:T(8,128)} copy(f32[4,2,8,64,1023]{4,2,3,1,0:T(8,128)} %get-tuple-element.10) | data formatting | bytes 33521664
  432.4 11.8 copy.116
  444.3 11.8 copy.117
  461.5 6.5 fusion.13
  469.7 10.9 fusion.34
  480.6 40.4 %all-to-all-done = f32[16,1,131072]{2,1,0:T(1,128)} async-done(((f32[16,1,131072]{2,1,0:T(1,128)}), f32[16,1,131072]{2,1,0:T(1,128)}, u32[]{:S(2)}, u32[]{:S(2)}) %all-to-all-start) | async-done | bytes 8388640 | tf_op jit(solution)/shard_map/all_to_all | solution.py:122
  521.5 25.1 %reduce = f32[16,131072]{1,0:T(8,128)} reduce(f32[16,1,131072]{2,1,0:T(1,128)} %all-to-all-done, f32[]{:T(128)} %broadcast.205), dimensions={1}, to_apply=%all_to_all.22.reduce_sub_computation | reduce | bytes 16777220 | tf_op jit(solution)/shard_map/all_to_all | solution.py:122
  546.7 223.7 %reshape.163 = f32[65536,1,4,8]{3,2,1,0:T(4,128)} reshape(f32[16,131072]{1,0:T(8,128)} %reduce) | data formatting | bytes 16777216
  770.4 100.1 %copy.84 = f32[4,1,8,16,4096]{4,2,3,0,1:T(8,128)} copy(f32[4,1,8,16,4096]{2,0,4,3,1:T(4,128)} %bitcast.12) | data formatting | bytes 16777216 | tf_op jit(solution)/shard_map/all_to_all | solution.py:122
  870.5 16.7 %fusion.14 = f32[4,1,128,4096]{2,3,0,1:T(8,128)} fusion(f32[128,128,1]{1,0,2:T(8,128)S(1)} %bitcast.83, f32[4,1,8,16,4096]{4,2,3,0,1:T(8,128)} %copy.84), kind=kOutput, calls=%fused_computation.23 | convolution fusion | flops 3221225472 | bytes 16842752 | tf_op jit(solution)/shard_map/mn,cgnq->cgmq/dot_general | solution.py:119
  887.3 10.3 copy.77
  897.6 14.6 %all-to-all-start.1 = ((f32[4,1,128,4096]{3,0,1,2:T(4,128)}), f32[4,1,128,4096]{3,0,1,2:T(4,128)}, u32[]{:S(2)}, u32[]{:S(2)}) async-start(f32[4,1,128,4096]{3,0,1,2:T(4,128)} %copy.77), calls=%async_computation.1 | async-start | bytes 16777216 | tf_op jit(solution)/shard_map/all_to_all | solution.py:125
  912.8 8.3 fusion.19
  924.9 17.8 %fusion.1 = f32[4,2,8,65536]{3,2,1,0:T(8,128)} fusion(f32[4,2,1,65536]{3,2,1,0:T(1,128)S(1)} %copy.61, f32[4,2,7,65536]{3,2,1,0:T(8,128)} %slice.88, f32[4,2,8,65536]{3,2,1,0:T(8,128)} %copy-done.2, f32[8]{0:T(128)S(1)} %add_convert_fusion, f32[8]{0:T(128)S(1)} %broadcast_add_fusion, f32[]{:T(128)} %bitcast), kind=kLoop, calls=%fused_computation.2 | loop fusion | flops 20971520 | bytes 50331716 | tf_op jit(solution)/shard_map/mul | solution.py:44
  942.7 151.9 %all-to-all-done.1 = f32[4,1,128,4096]{3,0,1,2:T(4,128)} async-done(((f32[4,1,128,4096]{3,0,1,2:T(4,128)}), f32[4,1,128,4096]{3,0,1,2:T(4,128)}, u32[]{:S(2)}, u32[]{:S(2)}) %all-to-all-start.1) | async-done | bytes 8388640 | tf_op jit(solution)/shard_map/all_to_all | solution.py:125
  1094.6 8.2 copy.119
  1103.0 8.2 copy.79
  1116.0 9.9 reshape.155
  1125.9 3.9 multiply_bitcast_fusion.2
  1133.1 25.6 %fusion.10 = (f32[4,8,64,1024]{3,2,1,0:T(8,128)}, f32[4,8,64,1024]{3,2,1,0:T(8,128)}) fusion(f32[4,1,8,64,1024]{4,2,3,1,0:T(8,128)} %get-tuple-element.5, f32[4,1,8,64,1024]{4,2,3,1,0:T(8,128)} %get-tuple-element.6, f32[1024]{0:T(1024)S(1)} %bitcast.84, f32[]{:T(128)} %bitcast.7, f32[4,1,8,64,1024]{4,3,2,0,1:T(8,128)S(1)} %bitcast.81, f32[]{:T(128)} %bitcast.11), kind=kLoop, calls=%fused_computation.16 | loop fusion | flops 10485760 | bytes 41947144 | tf_op jit(solution)/shard_map/mul | solution.py:78
  1158.8 61.4 %fusion.8 = f32[4,2,8,64,1024]{4,3,2,1,0:T(8,128)} fusion(f32[4,2,8,64,1024]{4,2,3,1,0:T(8,128)} %bitcast.73, f32[4,2,8,64,1023]{4,3,2,1,0:T(8,128)} %copy.115, f32[4,2,8,64,1023]{4,3,2,1,0:T(8,128)} %copy.116, f32[4,2,8,63,1024]{4,3,2,1,0:T(8,128)} %copy.117, f32[4,2,8,63,1024]{4,3,2,1,0:T(8,128)} %copy.118, f32[2,8,64,1024]{3,2,1,0:T(8,128)} %get-tuple-element.23, ...), kind=kLoop, calls=%fused_computation.10 | loop fusion | flops 113246208 | bytes 148345440 | tf_op jit(solution)/shard_map/mul | solution.py:90
  1220.1 14.6 %reshape.156 = f32[4,2,8,65536]{3,2,1,0:T(8,128)} reshape(f32[4,2,8,64,1024]{4,3,2,1,0:T(8,128)} %fusion.8) | data formatting | bytes 33554432 | tf_op jit(solution)/shard_map/reshape | solution.py:142
  (85 shorter events, 32.4 us)
Async XLA Ops:
  0.0 460.5 %copy-start = (f32[16]{0:T(128)S(1)}, f32[16]{0:T(128)}, u32[]{:S(2)}) copy-start(f32[16]{0:T(128)} %param.13) | copy-start | bytes 196
  12.3 6.2 copy-start.2
  331.7 7.1 slice-start.4
  331.7 189.3 %all-to-all-start = ((f32[16,1,131072]{2,1,0:T(1,128)}), f32[16,1,131072]{2,1,0:T(1,128)}, u32[]{:S(2)}, u32[]{:S(2)}) async-start(f32[16,1,131072]{2,1,0:T(1,128)} %reshape.162), calls=%async_computation | async-start | bytes 16777216 | tf_op jit(solution)/shard_map/all_to_all | solution.py:122
  341.5 579.7 %collective-permute-start = (f32[4,2,1,65536]{3,0,2,1:T(4,128)}, f32[4,2,1,65536]{3,0,2,1:T(4,128)}, u32[]{:S(2)}, u32[]{:S(2)}) collective-permute-start(f32[4,2,1,65536]{3,0,2,1:T(4,128)} %copy.60), channel_id=1, source_target_pairs={{1,0},{2,1},{3,2},{4,3},{5,4},{6,5},{7,6},{8,7},{9,8},{10,9},{11,1... | collective-permute-start | bytes 6291464 | tf_op jit(solution)/shard_map/ppermute | solution.py:16
  346.2 14.8 %copy-start.3 = (f32[1,2,8,65536]{3,2,1,0:T(8,128)}, f32[1,2,8,65536]{3,2,1,0:T(8,128)S(1)}, u32[]{:S(2)}) copy-start(f32[1,2,8,65536]{3,2,1,0:T(8,128)S(1)} %slice.98) | copy-start | bytes 12582916
  346.2 19.2 %slice-start = ((s8[16777216]{0:T(1024)(128)(4,1)}), s8[4194304]{0:T(1024)(128)(4,1)S(1)}, s32[]{:S(2)}) async-start(s8[16777216]{0:T(1024)(128)(4,1)} %bitcast.70), calls=%async_computation.2 | async-start | bytes 8388608
  346.2 19.2 %slice-start.1 = ((s8[16777216]{0:T(1024)(128)(4,1)}), s8[4194304]{0:T(1024)(128)(4,1)S(1)}, s32[]{:S(2)}) async-start(s8[16777216]{0:T(1024)(128)(4,1)} %bitcast.70), calls=%async_computation.3 | async-start | bytes 8388608
  346.2 19.2 %slice-start.2 = ((s8[16777216]{0:T(1024)(128)(4,1)}), s8[4194304]{0:T(1024)(128)(4,1)S(1)}, s32[]{:S(2)}) async-start(s8[16777216]{0:T(1024)(128)(4,1)} %bitcast.70), calls=%async_computation.4 | async-start | bytes 8388608
  346.3 19.2 %slice-start.3 = ((s8[16777216]{0:T(1024)(128)(4,1)}), s8[4194304]{0:T(1024)(128)(4,1)S(1)}, s32[]{:S(2)}) async-start(s8[16777216]{0:T(1024)(128)(4,1)} %bitcast.70), calls=%async_computation.5 | async-start | bytes 8388608
  414.0 30.2 %slice-start.5 = ((s8[16515072]{0:T(1024)(128)(4,1)}), s8[4194304]{0:T(1024)(128)(4,1)S(1)}, s32[]{:S(2)}) async-start(s8[16515072]{0:T(1024)(128)(4,1)} %bitcast.74), calls=%async_computation.7 | async-start | bytes 8388608
  414.0 30.2 %slice-start.6 = ((s8[16515072]{0:T(1024)(128)(4,1)}), s8[4194304]{0:T(1024)(128)(4,1)S(1)}, s32[]{:S(2)}) async-start(s8[16515072]{0:T(1024)(128)(4,1)} %bitcast.74), calls=%async_computation.8 | async-start | bytes 8388608
  432.4 11.8 slice-start.7
  432.4 11.8 slice-start.8
  444.2 11.8 copy-start.14
  444.2 11.8 copy-start.16
  444.2 15.5 %copy-start.15 = (s32[128]{0:T(128)S(1)}, s32[128]{0:T(128)}, u32[]{:S(2)}) copy-start(s32[128]{0:T(128)} %param.15) | copy-start | bytes 1540
  444.2 16.3 %copy-start.13 = (s32[1024]{0:T(1024)S(1)}, s32[1024]{0:T(1024)}, u32[]{:S(2)}) copy-start(s32[1024]{0:T(1024)} %param.14) | copy-start | bytes 12292
  444.2 23.8 %copy-start.6 = (s32[8]{0:T(128)S(1)}, s32[8]{0:T(128)}, u32[]{:S(2)}) copy-start(s32[8]{0:T(128)} %param.16) | copy-start | bytes 100
  897.6 197.0 %all-to-all-start.1 = ((f32[4,1,128,4096]{3,0,1,2:T(4,128)}), f32[4,1,128,4096]{3,0,1,2:T(4,128)}, u32[]{:S(2)}, u32[]{:S(2)}) async-start(f32[4,1,128,4096]{3,0,1,2:T(4,128)} %copy.77), calls=%async_computation.1 | async-start | bytes 16777216 | tf_op jit(solution)/shard_map/all_to_all | solution.py:125
  1111.2 18.6 %copy-start.7 = (f32[2]{0:T(128)S(1)}, f32[2]{0:T(128)}, u32[]{:S(2)}) copy-start(f32[2]{0:T(128)} %constant.52.clone) | copy-start | bytes 28
  1116.0 17.0 %copy-start.5 = (f32[1,1024]{1,0:T(1,128)S(1)}, f32[1,1024]{1,0:T(1,128)}, u32[]{:S(2)}) copy-start(f32[1,1024]{1,0:T(1,128)} %fusion.21) | copy-start | bytes 12292
  1125.9 7.1 slice-start.9
  1129.8 3.2 slice-start.10
  1133.0 25.7 %copy-start.4 = (f32[1024]{0:T(1024)S(1)}, f32[1024]{0:T(1024)}, u32[]{:S(2)}) copy-start(f32[1024]{0:T(1024)} %iota_add_fusion) | copy-start | bytes 12292
  1133.0 25.7 %copy-start.8 = (f32[4]{0:T(128)S(1)}, f32[4]{0:T(128)}, u32[]{:S(2)}) copy-start(f32[4]{0:T(128)} %compare_convert_fusion.4) | copy-start | bytes 52
  1133.0 25.7 %copy-start.9 = (f32[4]{0:T(128)S(1)}, f32[4]{0:T(128)}, u32[]{:S(2)}) copy-start(f32[4]{0:T(128)} %get-tuple-element.24) | copy-start | bytes 52
  1133.0 25.7 %copy-start.10 = (f32[4]{0:T(128)S(1)}, f32[4]{0:T(128)}, u32[]{:S(2)}) copy-start(f32[4]{0:T(128)} %get-tuple-element.25) | copy-start | bytes 52
  1133.0 25.7 %copy-start.11 = (f32[64]{0:T(128)S(1)}, f32[64]{0:T(128)}, u32[]{:S(2)}) copy-start(f32[64]{0:T(128)} %get-tuple-element.26) | copy-start | bytes 772
  1133.1 25.7 %copy-start.12 = (f32[64]{0:T(128)S(1)}, f32[64]{0:T(128)}, u32[]{:S(2)}) copy-start(f32[64]{0:T(128)} %get-tuple-element.27) | copy-start | bytes 772
  1158.7 76.0 %copy-start.1 = (f32[16]{0:T(128)S(1)}, f32[16]{0:T(128)}, u32[]{:S(2)}) copy-start(f32[16]{0:T(128)} %param.13) | copy-start | bytes 196
where the time goes:
time: 1250 us; the launch traced here: 1230 us
  local copies, waits for them, and re-layouts  830 us (66%)
  waiting for transfers between devices  192 us (15%)
  other arithmetic  164 us (13%)
  matrix products  24.3 us (2%)
  starting transfers between devices  23.9 us (2%)
    unnamed x61, local copies, waits for them, and re-layouts  517 us
    all_to_all x1, waiting for transfers between devices, local(): lax.all_to_all(summed, 'slab', split_axis=2, concat_axis=3, tiled=True)  152 us
    all_to_all x2, local copies, waits for them, and re-layouts, local(): lax.all_to_all(solution_tensor[:, 1:2], 'slab', split_axis=3, concat_axis...  101 us
    slice x2, local copies, waits for them, and re-layouts, local(): solution_tensor[:, 1:2]  89.6 us
    mul x1, other arithmetic, lattice_rates(): return inside * (total + sources)  61.4 us
    all_to_all x1, waiting for transfers between devices, local(): lax.all_to_all(solution_tensor[:, 1:2], 'slab', split_axis=3, concat_axis...  40.4 us
    mul x1, other arithmetic, lattice_rates(): gene_sign * (silencing_rate * expressing - kon_grid * silent)  25.6 us
    all_to_all x1, other arithmetic, local(): lax.all_to_all(solution_tensor[:, 1:2], 'slab', split_axis=3, concat_axis...  25.1 us
  transfers between devices with their start and end apart: 3, of which 2 were waited for; matrix products, arithmetic and copies ran while one was open for 44% of the time, Pallas kernels for 0%

commit v1 on v0

v1 whole, which is shorter than its diff:
```python
import functools

import jax
import jax.numpy as jnp
from jax import lax
from jax.experimental import pallas as pl
from jax.experimental.pallas import tpu as pltpu
from jax.sharding import PartitionSpec as P

P2 = 1024
nominal_coefficient_basis = (2.0, 0.02, 1.0, 0.01, 0.02, 0.03, 0.002)
section_step = 0.125
PLANES = 8
VMEM_LIMIT = 48 * 1024 * 1024
HIGHEST = lax.Precision.HIGHEST


def shifted(value, axis, steps):
    count = lax.axis_size(axis)
    first, last = (max(0, -steps), min(count, count - steps))
    return lax.ppermute(value, axis, [(source, source + steps) for source in range(first, last)])


def episode_share_stencil(measured_outbreak_frequencies, stencil_breadth):
    episode_extents = jnp.arange(stencil_breadth, dtype=jnp.int32)
    episode_shares = measured_outbreak_frequencies.astype(jnp.float32) * (
        episode_extents >= 1
    ).astype(jnp.float32)
    episode_shares = episode_shares / jnp.sum(episode_shares)
    backward_difference = episode_extents[:, None] - episode_extents[None, :]
    single_selector = (backward_difference[:, :, None] == episode_extents[None, None, :]).astype(
        jnp.float32
    )
    return jnp.dot(single_selector, episode_shares, precision=HIGHEST)


def kon_rates(unlocking_coefficients_by_grade, repression_grade_by_abundance):
    levels = jnp.arange(unlocking_coefficients_by_grade.shape[0], dtype=jnp.int32)
    single_selector = (repression_grade_by_abundance[:, None] == levels[None, :]).astype(
        jnp.float32
    )
    return jnp.dot(single_selector, unlocking_coefficients_by_grade, precision=HIGHEST)


def on_state(start, velocity, bound, component, blocks):
    _, _, rows, cells = start.shape
    width = cells // blocks
    per_step = max(1, min(blocks, 8192 // width))
    planes = width // P2 if width >= P2 else 1

    def kernel(bound_ref, start_ref, velocity_ref, out_ref):
        step = pl.program_id(0)
        value = start_ref[...] + section_step * velocity_ref[...]
        cell = step * (per_step * width) + lax.broadcasted_iota(jnp.int32, value.shape, 1)
        value = jnp.where((cell // P2) < bound_ref[:, 0:1], value, 0.0)
        for part in range(per_step):
            out_ref[part] = value[:, part * width : (part + 1) * width]

    spec = pl.BlockSpec((None, None, rows, per_step * width), lambda j: (component, 1, 0, j))
    return pl.pallas_call(
        kernel,
        grid=(blocks // per_step,),
        in_specs=[pl.BlockSpec((rows, 128), lambda j: (0, 0)), spec, spec],
        out_specs=pl.BlockSpec((per_step, rows, width), lambda j: (j, 0, 0)),
        out_shape=jax.ShapeDtypeStruct((blocks, rows, width), jnp.float32),
        compiler_params=pltpu.CompilerParams(vmem_limit_bytes=VMEM_LIMIT),
        cost_estimate=pl.CostEstimate(
            flops=3 * rows * cells, bytes_accessed=12 * rows * cells, transcendentals=0
        ),
    )(bound, start, velocity)


def partial_slope(start, velocity, halo, rates, bound, row_rates, diagonals, columns):
    comps, genes, rows, cells = start.shape
    firsts = cells // P2
    steps = firsts // PLANES

    def kernel(
        rate_ref,
        bound_ref,
        row_ref,
        diagonal_ref,
        column_ref,
        start_ref,
        velocity_ref,
        start_low,
        velocity_low,
        start_high,
        velocity_high,
        halo_ref,
        out_ref,
        state,
    ):
        step = pl.program_id(0)
        off, decay1, make2 = rate_ref[2], rate_ref[4], rate_ref[5]
        first_plane = step * PLANES
        bound_column = bound_ref[:, 0:1]

        def masked(plane, value):
            return jnp.where((bound_column > plane) & (plane >= 0), value, 0.0)

        for comp in range(comps):
            for gene in range(genes):
                state[0, comp, gene] = masked(
                    first_plane - 1,
                    start_low[comp, gene] + section_step * velocity_low[comp, gene],
                )
                high = start_high[comp, gene] + section_step * velocity_high[comp, gene]
                state[PLANES + 1, comp, gene] = jnp.where(
                    first_plane + PLANES < firsts, masked(first_plane + PLANES, high), 0.0
                )

        @pl.loop(0, PLANES)
        def _(plane):
            lanes = pl.ds(pl.multiple_of(plane * P2, P2), P2)
            for comp in range(comps):
                for gene in range(genes):
                    state[plane + 1, comp, gene] = masked(
                        first_plane + plane,
                        start_ref[comp, gene, :, lanes]
                        + section_step * velocity_ref[comp, gene, :, lanes],
                    )

        @pl.loop(0, PLANES)
        def _(plane):
            lanes = pl.ds(pl.multiple_of(plane * P2, P2), P2)
            count = (first_plane + plane).astype(jnp.float32)
            inside = bound_column > first_plane + plane
            trans_m = row_ref[:, 0:1]
            mdecay_up = row_ref[:, 128:129]
            own = -count * (decay1 + make2)
            above_rate = decay1 * (count + 1.0)
            made = (make2 * count) * column_ref[1:2, :]
            removed = column_ref[2:3, :]
            kon = column_ref[0:1, :]
            last_row = lax.broadcasted_iota(jnp.int32, (rows, P2), 0) == rows - 1
            for comp in range(comps):
                silent = state[plane + 1, comp, 0]
                active = state[plane + 1, comp, 1]
                for gene in range(genes):
                    value = silent if gene == 0 else active
                    lower = state[plane, comp, gene]
                    total = (diagonal_ref[gene] + own) * value
                    total = total + trans_m * lower
                    total = total + above_rate * state[plane + 2, comp, gene]
                    total = total + made * pltpu.roll(value, 1, 1)
                    total = total + removed * pltpu.roll(value, P2 - 1, 1)
                    if gene == 0:
                        total = total + off * active
                        beyond = jnp.where(
                            last_row,
                            halo_ref[comp : comp + 1, lanes],
                            pltpu.roll(value, rows - 1, 0),
                        )
                        total = total + mdecay_up * beyond
                    else:
                        total = total + kon * silent
                    if comp == 2:
                        total = total + trans_m * (
                            state[plane, 0, gene] - state[plane + 1, 0, gene]
                        )
                    if comp == 3:
                        source = off * state[plane + 1, 0, 1]
                        total = total + source if gene == 0 else total - source
                    out_ref[comp, gene, :, lanes] = jnp.where(inside, total, 0.0)

    def whole(shape):
        return pl.BlockSpec(shape, lambda i: (0,) * len(shape))

    main = pl.BlockSpec((comps, genes, rows, PLANES * P2), lambda i: (0, 0, 0, i))
    low = pl.BlockSpec((comps, genes, rows, P2), lambda i: (0, 0, 0, jnp.maximum(i * PLANES - 1, 0)))
    high = pl.BlockSpec(
        (comps, genes, rows, P2), lambda i: (0, 0, 0, jnp.minimum((i + 1) * PLANES, firsts - 1))
    )
    return pl.pallas_call(
        kernel,
        grid=(steps,),
        in_specs=[
            pl.BlockSpec(memory_space=pltpu.SMEM),
            whole((rows, 128)),
            whole((rows, 256)),
            whole((genes, rows, P2)),
            whole((8, P2)),
            main,
            main,
            low,
            low,
            high,
            high,
            pl.BlockSpec((comps, PLANES * P2), lambda i: (0, i)),
        ],
        out_specs=main,
        out_shape=jax.ShapeDtypeStruct(start.shape, jnp.float32),
        scratch_shapes=[pltpu.VMEM((PLANES + 2, comps, genes, rows, P2), jnp.float32)],
        compiler_params=pltpu.CompilerParams(vmem_limit_bytes=VMEM_LIMIT),
        cost_estimate=pl.CostEstimate(
            flops=30 * start.size, bytes_accessed=16 * start.size, transcendentals=0
        ),
    )(rates, bound, row_rates, diagonals, columns, start, velocity, start, velocity, start, velocity, halo)


def add_rows(slope, returned, bound, component):
    _, _, rows, cells = slope.shape
    blocks, _, width = returned.shape
    per_step = max(1, min(blocks, 8192 // width))

    def kernel(bound_ref, slope_ref, returned_ref, out_ref):
        step = pl.program_id(0)
        for part in range(per_step):
            cell = (step * per_step + part) * width + lax.broadcasted_iota(
                jnp.int32, (rows, width), 1
            )
            lanes = slice(part * width, (part + 1) * width)
            out_ref[:, lanes] = slope_ref[:, lanes] + jnp.where(
                (cell // P2) < bound_ref[:, 0:1], returned_ref[part], 0.0
            )

    spec = pl.BlockSpec((None, None, rows, per_step * width), lambda j: (component, 1, 0, j))
    return pl.pallas_call(
        kernel,
        grid=(blocks // per_step,),
        in_specs=[
            pl.BlockSpec((rows, 128), lambda j: (0, 0)),
            spec,
            pl.BlockSpec((per_step, rows, width), lambda j: (j, 0, 0)),
        ],
        out_specs=spec,
        out_shape=jax.ShapeDtypeStruct(slope.shape, jnp.float32),
        input_output_aliases={1: 0},
        compiler_params=pltpu.CompilerParams(vmem_limit_bytes=VMEM_LIMIT),
        cost_estimate=pl.CostEstimate(
            flops=2 * rows * cells, bytes_accessed=12 * rows * cells, transcendentals=0
        ),
    )(bound, slope, returned)


def local(
    starting_joint_sensitivities,
    former_section_velocity,
    nominal_coefficient_factors,
    unlocking_coefficients_by_grade,
    repression_grade_by_abundance,
    measured_outbreak_frequencies,
    upper_bounds_per_abundance,
):
    start, velocity = starting_joint_sensitivities, former_section_velocity
    comps, genes, rows, cells = start.shape
    blocks = lax.axis_size("slab")
    width = cells // blocks
    breadth = measured_outbreak_frequencies.shape[0]
    rates = nominal_coefficient_factors * jnp.array(nominal_coefficient_basis, dtype=jnp.float32)
    burst, trans, off, mdecay, decay1, make2, decay2 = [rates[place] for place in range(7)]
    bound = jnp.broadcast_to(upper_bounds_per_abundance[:, None], (rows, 128))

    order = (2, 3, 0, 1)
    arrived = {}
    for comp in order:
        sent = on_state(start, velocity, bound, comp, blocks)
        came = lax.all_to_all(sent, "slab", split_axis=0, concat_axis=0, tiled=True)
        arrived[comp] = came.reshape(breadth, width)

    first_index = jnp.arange(cells, dtype=jnp.int32) // P2
    lowest = start[:, 0, 0, :] + section_step * velocity[:, 0, 0, :]
    lowest = jnp.where(first_index[None, :] < upper_bounds_per_abundance[0], lowest, 0.0)
    halo = shifted(lowest, "slab", -1)

    first_row = lax.axis_index("slab") * rows
    m_count = (first_row + jnp.arange(rows, dtype=jnp.int32)).astype(jnp.float32)
    c_count = jnp.arange(P2, dtype=jnp.float32)
    kon = kon_rates(unlocking_coefficients_by_grade, repression_grade_by_abundance)
    row_rates = jnp.concatenate(
        [
            jnp.broadcast_to((trans * m_count)[:, None], (rows, 128)),
            jnp.broadcast_to((mdecay * (m_count + 1.0))[:, None], (rows, 128)),
        ],
        axis=1,
    )
    shared = -((trans * m_count)[:, None] + (decay2 * c_count)[None, :])
    diagonals = jnp.stack(
        [shared - (mdecay * m_count)[:, None] - kon[None, :], shared - off], axis=0
    )
    columns = jnp.zeros((8, P2), jnp.float32)
    columns = columns.at[0].set(kon)
    columns = columns.at[1].set((c_count >= 1.0).astype(jnp.float32))
    columns = columns.at[2].set(jnp.where(c_count < P2 - 1.0, decay2 * (c_count + 1.0), 0.0))
    slope = partial_slope(start, velocity, halo, rates, bound, row_rates, diagonals, columns)

    unit = jnp.eye(breadth, dtype=jnp.float32)
    m_all = jnp.arange(breadth, dtype=jnp.float32)
    episodes = burst * (episode_share_stencil(measured_outbreak_frequencies, breadth) - unit)
    removal = mdecay * (
        (m_all + 1.0)[:, None] * jnp.eye(breadth, k=1, dtype=jnp.float32) - m_all[:, None] * unit
    )
    matrix = episodes + removal

    returned = {}
    for comp in order:
        total = jnp.dot(matrix, arrived[comp], precision=HIGHEST)
        if comp == 1:
            total = total + jnp.dot(episodes, arrived[0], precision=HIGHEST)
        returned[comp] = lax.all_to_all(
            total.reshape(blocks, rows, width), "slab", split_axis=0, concat_axis=0, tiled=True
        )
    for comp in order:
        slope = add_rows(slope, returned[comp], bound, comp)
    return slope


def solution(mesh):
    placed = (
        P("ens", None, "slab", None),
        P("ens", None, "slab", None),
        P("ens"),
        P("ens"),
        P(),
        P(),
        P("slab"),
    )
    return jax.shard_map(
        local, mesh=mesh, in_specs=placed, out_specs=P("ens", None, "slab", None), check_vma=False
    )
```

time: 1250 us -> 498 us (0.40); the launches traced: 1230 us -> 496 us
  local copies, waits for them, and re-layouts: 830 us -> 12.3 us
  other arithmetic: 164 us -> 8.39 us
  waiting for transfers between devices: 192 us -> 315 us
  Pallas kernels: 0 us -> 83 us
  starting transfers between devices: 23.9 us -> 43.2 us
    unnamed x61 -> x18, local copies, waits for them, and re-layouts: 517 us -> 1.43 us
    slice x14 -> x3, local copies, waits for them, and re-layouts: 157 us -> 9.74 us  [the longest x2 9.07 us: local(): lowest = start[:, 0, 0, :] + section_step * velocity[:, 0, 0, :]]
    mul x9 -> x3, other arithmetic: 133 us -> 1.9 us  [the longest x1 0.69 us: local(): mdecay * (m_count + 1.0)]
    all_to_all x4 -> x0, local copies, waits for them, and re-layouts: 117 us -> none  [the longest x2 101 us: local(): lax.all_to_all(solution_tensor[:, 1:2], 'slab', split_axis=3, concat_axis...]
    pallas_call x0 -> x9, Pallas kernels: none -> 83 us  [the longest x4 28.1 us: on_state(): pl.pallas_call(kernel, grid=(blocks // per_step,), in_specs=[pl.BlockSpec...]
    all_to_all x2 -> x8, waiting for transfers between devices: 192 us -> 267 us  [the longest x4 155 us: local(): came = lax.all_to_all(sent, 'slab', split_axis=0, concat_axis=0, tiled=True)]
    ppermute x1, waiting for transfers between devices: 0.01 us -> 47.8 us  [shifted(): lax.ppermute(value, axis, [(source, source + steps) for source in range(f...]
    all_to_all x1 -> x0, other arithmetic: 25.1 us -> none  [local(): lax.all_to_all(solution_tensor[:, 1:2], 'slab', split_axis=3, concat_axis...]
  transfers between devices with their start and end apart: 3 -> 9, of which waited for: 2 -> 8; matrix products, arithmetic and copies ran while one was open for 44% -> 11% of each run, Pallas kernels for 0% -> 14%
where the time goes in v1:
time: 498 us; the launch traced here: 496 us
  waiting for transfers between devices  315 us (63%)
  Pallas kernels  83 us (17%)
  starting transfers between devices  43.2 us (9%)
  matrix products  34.2 us (7%)
  local copies, waits for them, and re-layouts  12.3 us (2%)
  other arithmetic  8.39 us (2%)
    all_to_all x4, waiting for transfers between devices, local(): came = lax.all_to_all(sent, 'slab', split_axis=0, concat_axis=0, tiled=True)  155 us
    all_to_all x4, waiting for transfers between devices, local(): lax.all_to_all(total.reshape(blocks, rows, width), 'slab', split_axis=0,...  112 us
    ppermute x1, waiting for transfers between devices, shifted(): lax.ppermute(value, axis, [(source, source + steps) for source in range(f...  47.8 us
    pallas_call x4, Pallas kernels, on_state(): pl.pallas_call(kernel, grid=(blocks // per_step,), in_specs=[pl.BlockSpec...  28.1 us
    pallas_call x1, Pallas kernels, partial_slope(): pl.pallas_call(kernel, grid=(steps,), in_specs=[pl.BlockSpec(memory_space...  27.9 us
    pallas_call x4, Pallas kernels, add_rows(): pl.pallas_call(kernel, grid=(blocks // per_step,), in_specs=[pl.BlockSpec...  27.1 us
    dot_general x4, matrix products, local(): total = jnp.dot(matrix, arrived[comp], precision=HIGHEST)  21.7 us
    all_to_all x4, starting transfers between devices, local(): came = lax.all_to_all(sent, 'slab', split_axis=0, concat_axis=0, tiled=True)  21.3 us
  transfers between devices with their start and end apart: 9, of which 8 were waited for; matrix products, arithmetic and copies ran while one was open for 11% of the time, Pallas kernels for 14%

profile of v1, /device:TPU:11, one launch (start us, length us, event | category | flops | bytes accessed | tf_op | source)
XLA Modules:
  0.0 496.1 jit_solution(15995754804992781844)
XLA Ops:
  0.7 7.0 %shard_map.83 = f32[16,8,4096]{2,1,0:T(8,128)} custom-call(s32[8,128]{1,0:T(8,128)S(1)} %broadcast_in_dim.19.bound_ref, f32[4,2,8,65536]{3,2,1,0:T(8,128)} %start_ref.9, f32[4,2,8,65536]{3,2,1,0:T(8,128)} %velocity_ref.9), custom_call_target="tpu_custom_call" | custom-call | flops 1572864 | bytes 6291456 | tf_op jit(solution)/shard_map/pallas_call | solution.py:60
  7.7 6.6 %all-to-all-start = ((f32[16,8,4096]{2,1,0:T(8,128)}), f32[16,8,4096]{2,1,0:T(8,128)}, u32[]{:S(2)}, u32[]{:S(2)}) async-start(f32[16,8,4096]{2,1,0:T(8,128)} %shard_map.83), calls=%async_computation | async-start | bytes 4194304 | tf_op jit(solution)/shard_map/all_to_all | solution.py:259
  14.3 7.0 %shard_map.85 = f32[16,8,4096]{2,1,0:T(8,128)} custom-call(s32[8,128]{1,0:T(8,128)S(1)} %broadcast_in_dim.19.bound_ref, f32[4,2,8,65536]{3,2,1,0:T(8,128)} %start_ref.9, f32[4,2,8,65536]{3,2,1,0:T(8,128)} %velocity_ref.9), custom_call_target="tpu_custom_call" | custom-call | flops 1572864 | bytes 6291456 | tf_op jit(solution)/shard_map/pallas_call | solution.py:60
  21.3 40.5 %all-to-all-done = f32[16,8,4096]{2,1,0:T(8,128)} async-done(((f32[16,8,4096]{2,1,0:T(8,128)}), f32[16,8,4096]{2,1,0:T(8,128)}, u32[]{:S(2)}, u32[]{:S(2)}) %all-to-all-start) | async-done | bytes 2097184 | tf_op jit(solution)/shard_map/all_to_all | solution.py:259
  61.8 4.9 all-to-all-start.2
  66.7 7.0 %shard_map.87 = f32[16,8,4096]{2,1,0:T(8,128)} custom-call(s32[8,128]{1,0:T(8,128)S(1)} %broadcast_in_dim.19.bound_ref, f32[4,2,8,65536]{3,2,1,0:T(8,128)} %start_ref.9, f32[4,2,8,65536]{3,2,1,0:T(8,128)} %velocity_ref.9), custom_call_target="tpu_custom_call" | custom-call | flops 1572864 | bytes 6291456 | tf_op jit(solution)/shard_map/pallas_call | solution.py:60
  73.7 40.5 %all-to-all-done.2 = f32[16,8,4096]{2,1,0:T(8,128)} async-done(((f32[16,8,4096]{2,1,0:T(8,128)}), f32[16,8,4096]{2,1,0:T(8,128)}, u32[]{:S(2)}, u32[]{:S(2)}) %all-to-all-start.2) | async-done | bytes 2097184 | tf_op jit(solution)/shard_map/all_to_all | solution.py:259
  114.3 4.9 all-to-all-start.4
  119.2 7.1 %shard_map.89 = f32[16,8,4096]{2,1,0:T(8,128)} custom-call(s32[8,128]{1,0:T(8,128)S(1)} %broadcast_in_dim.19.bound_ref, f32[4,2,8,65536]{3,2,1,0:T(8,128)} %start_ref.9, f32[4,2,8,65536]{3,2,1,0:T(8,128)} %velocity_ref.9), custom_call_target="tpu_custom_call" | custom-call | flops 1572864 | bytes 6291456 | tf_op jit(solution)/shard_map/pallas_call | solution.py:60
  126.3 40.4 %all-to-all-done.4 = f32[16,8,4096]{2,1,0:T(8,128)} async-done(((f32[16,8,4096]{2,1,0:T(8,128)}), f32[16,8,4096]{2,1,0:T(8,128)}, u32[]{:S(2)}, u32[]{:S(2)}) %all-to-all-start.4) | async-done | bytes 2097184 | tf_op jit(solution)/shard_map/all_to_all | solution.py:259
  166.7 4.9 all-to-all-start.6
  172.9 6.5 %fusion = f32[1,128,128]{2,0,1:T(1,128)S(1)} fusion(s32[128,128]{1,0:T(8,128)S(1)} %iota_subtract_fusion, f32[]{:T(128)} %fusion.30, s32[128]{0:T(128)S(1)} %copy-done.7), kind=kOutput, calls=%fused_computation.1 | convolution fusion | flops 27263488 | bytes 131588 | tf_op jit(solution)/shard_map/dot_general | solution.py:34
  179.4 6.2 %fusion.7 = f32[16,8,4096]{2,1,0:T(8,128)} fusion(f32[16,8,4096]{2,1,0:T(8,128)} %all-to-all-done, f32[128,128]{1,0:T(8,128)S(1)} %bitcast.49, f32[128]{0:T(128)S(1)} %iota_add_fusion, s32[128]{0:T(128)S(1)} %iota_add_fusion.1, f32[]{:T(128)} %bitcast.1, f32[]{:T(128)} %bitcast.8), kind=kOutput, calls=%fused_computation.9 | convolution fusion | flops 805470208 | bytes 4260872 | tf_op jit(solution)/shard_map/dot_general | solution.py:298
  185.6 33.4 %all-to-all-done.6 = f32[16,8,4096]{2,1,0:T(8,128)S(1)} async-done(((f32[16,8,4096]{2,1,0:T(8,128)}), f32[16,8,4096]{2,1,0:T(8,128)S(1)}, u32[]{:S(2)}, u32[]{:S(2)}) %all-to-all-start.6) | async-done | bytes 2097184 | tf_op jit(solution)/shard_map/all_to_all | solution.py:259
  220.4 4.9 all-to-all-start.1
  225.3 6.2 %fusion.5 = f32[16,8,4096]{2,1,0:T(8,128)} fusion(f32[16,8,4096]{2,1,0:T(8,128)} %all-to-all-done.2, f32[128,128]{1,0:T(8,128)S(1)} %bitcast.50, f32[128]{0:T(128)S(1)} %iota_add_fusion, s32[128]{0:T(128)S(1)} %iota_add_fusion.1, f32[]{:T(128)} %bitcast.1, f32[]{:T(128)} %bitcast.8), kind=kOutput, calls=%fused_computation.7 | convolution fusion | flops 805470208 | bytes 4260872 | tf_op jit(solution)/shard_map/dot_general | solution.py:298
  231.5 41.2 %all-to-all-done.1.returned_ref = f32[16,8,4096]{2,1,0:T(8,128)S(1)} async-done(((f32[16,8,4096]{2,1,0:T(8,128)}), f32[16,8,4096]{2,1,0:T(8,128)S(1)}, u32[]{:S(2)}, u32[]{:S(2)}) %all-to-all-start.1) | async-done | bytes 2097184 | tf_op jit(solution)/shard_map/all_to_all | solution.py:301
  272.7 4.9 all-to-all-start.3
  277.7 6.1 %fusion.3 = f32[16,8,4096]{2,1,0:T(8,128)} fusion(f32[16,8,4096]{2,1,0:T(8,128)} %all-to-all-done.4, f32[128,128]{1,0:T(8,128)S(1)} %bitcast.51, f32[128]{0:T(128)S(1)} %iota_add_fusion, s32[128]{0:T(128)S(1)} %iota_add_fusion.1, f32[]{:T(128)} %bitcast.1, f32[]{:T(128)} %bitcast.8), kind=kOutput, calls=%fused_computation.5 | convolution fusion | flops 805470208 | bytes 4260872 | tf_op jit(solution)/shard_map/dot_general | solution.py:298
  283.8 41.4 %all-to-all-done.3.returned_ref = f32[16,8,4096]{2,1,0:T(8,128)} async-done(((f32[16,8,4096]{2,1,0:T(8,128)}), f32[16,8,4096]{2,1,0:T(8,128)}, u32[]{:S(2)}, u32[]{:S(2)}) %all-to-all-start.3) | async-done | bytes 2097184 | tf_op jit(solution)/shard_map/all_to_all | solution.py:301
  325.2 4.9 all-to-all-start.5
  334.2 5.0 %slice.74 = f32[4,1,1,65536]{3,2,1,0:T(1,128)} slice(f32[4,2,8,65536]{3,2,1,0:T(8,128)} %velocity_ref.9), slice={[0:4], [0:1], [0:1], [0:65536]} | slice | bytes 2097152 | tf_op jit(solution)/shard_map/slice | solution.py:263
  342.6 5.6 %fusion.1 = f32[16,8,4096]{2,1,0:T(8,128)} fusion(f32[128,4096]{1,0:T(8,128)S(1)} %fusion.9, f32[16,8,4096]{2,1,0:T(8,128)} %all-to-all-done.4, f32[128,128]{1,0:T(8,128)S(1)} %bitcast.53, f32[]{:T(128)} %bitcast.8), kind=kOutput, calls=%fused_computation.3 | convolution fusion | flops 805896192 | bytes 6356996 | tf_op jit(solution)/shard_map/dot_general | solution.py:300
  348.1 29.5 %all-to-all-done.5.returned_ref = f32[16,8,4096]{2,1,0:T(8,128)} async-done(((f32[16,8,4096]{2,1,0:T(8,128)}), f32[16,8,4096]{2,1,0:T(8,128)}, u32[]{:S(2)}, u32[]{:S(2)}) %all-to-all-start.5) | async-done | bytes 2097184 | tf_op jit(solution)/shard_map/all_to_all | solution.py:301
  377.6 4.9 all-to-all-start.7
  382.5 4.4 fusion.14
  393.4 47.8 %collective-permute-done.halo_ref = f32[4,65536]{1,0:T(4,128)S(1)} collective-permute-done((f32[4,65536]{1,0:T(4,128)}, f32[4,65536]{1,0:T(4,128)S(1)}, u32[]{:S(2)}, u32[]{:S(2)}) %collective-permute-start) | collective-permute-done | bytes 1048608 | tf_op jit(solution)/shard_map/ppermute | solution.py:21
  441.2 27.9 %shard_map.82.slope_ref = f32[4,2,8,65536]{3,2,1,0:T(8,128)} custom-call(f32[7]{0:T(128)S(1)} %mul.95.rate_ref, s32[8,128]{1,0:T(8,128)S(1)} %broadcast_in_dim.19.bound_ref, f32[8,256]{1,0:T(8,128)S(1)} %pad_maximum_fusion.1.row_ref, f32[2,8,1024]{2,1,0:T(8,128)S(1)} %pad_maximum_fusion.diagonal_ref, f32[8,1024]{1,0:T(8,128)S(1)} %scatter.14.column_ref, ...), custom_call_target="tpu_custom_call" | custom-call | flops 125829120 | bytes 67108864 | tf_op jit(solution)/shard_map/pallas_call | solution.py:175
  469.0 6.5 %shard_map.84.slope_ref = f32[4,2,8,65536]{3,2,1,0:T(8,128)} custom-call(s32[8,128]{1,0:T(8,128)S(1)} %broadcast_in_dim.19.bound_ref, f32[4,2,8,65536]{3,2,1,0:T(8,128)} %shard_map.82.slope_ref, f32[16,8,4096]{2,1,0:T(8,128)S(1)} %all-to-all-done.1.returned_ref), custom_call_target="tpu_custom_call", output_to_operand_aliasing={{}: (1, {})} | custom-call | flops 1048576 | bytes 6291456 | tf_op jit(solution)/shard_map/pallas_call | solution.py:219
  475.6 6.8 %shard_map.86.slope_ref = f32[4,2,8,65536]{3,2,1,0:T(8,128)} custom-call(s32[8,128]{1,0:T(8,128)S(1)} %broadcast_in_dim.19.bound_ref, f32[4,2,8,65536]{3,2,1,0:T(8,128)} %shard_map.84.slope_ref, f32[16,8,4096]{2,1,0:T(8,128)} %all-to-all-done.3.returned_ref), custom_call_target="tpu_custom_call", output_to_operand_aliasing={{}: (1, {})} | custom-call | flops 1048576 | bytes 6291456 | tf_op jit(solution)/shard_map/pallas_call | solution.py:219
  482.4 6.8 %shard_map.88.slope_ref = f32[4,2,8,65536]{3,2,1,0:T(8,128)} custom-call(s32[8,128]{1,0:T(8,128)S(1)} %broadcast_in_dim.19.bound_ref, f32[4,2,8,65536]{3,2,1,0:T(8,128)} %shard_map.86.slope_ref, f32[16,8,4096]{2,1,0:T(8,128)} %all-to-all-done.5.returned_ref), custom_call_target="tpu_custom_call", output_to_operand_aliasing={{}: (1, {})} | custom-call | flops 1048576 | bytes 6291456 | tf_op jit(solution)/shard_map/pallas_call | solution.py:219
  489.2 6.9 %shard_map.90 = f32[4,2,8,65536]{3,2,1,0:T(8,128)} custom-call(s32[8,128]{1,0:T(8,128)S(1)} %broadcast_in_dim.19.bound_ref, f32[4,2,8,65536]{3,2,1,0:T(8,128)} %shard_map.88.slope_ref, f32[16,8,4096]{2,1,0:T(8,128)} %all-to-all-done.7.returned_ref), custom_call_target="tpu_custom_call", output_to_operand_aliasing={{}: (1, {})} | custom-call | flops 1048576 | bytes 6291456 | tf_op jit(solution)/shard_map/pallas_call | solution.py:219
  (44 shorter events, 17.2 us)
Async XLA Ops:
  0.0 389.2 %copy-start = (f32[16]{0:T(128)S(1)}, f32[16]{0:T(128)}, u32[]{:S(2)}) copy-start(f32[16]{0:T(128)} %param.17) | copy-start | bytes 196
  7.7 54.1 %all-to-all-start = ((f32[16,8,4096]{2,1,0:T(8,128)}), f32[16,8,4096]{2,1,0:T(8,128)}, u32[]{:S(2)}, u32[]{:S(2)}) async-start(f32[16,8,4096]{2,1,0:T(8,128)} %shard_map.83), calls=%async_computation | async-start | bytes 4194304 | tf_op jit(solution)/shard_map/all_to_all | solution.py:259
  61.8 52.4 %all-to-all-start.2 = ((f32[16,8,4096]{2,1,0:T(8,128)}), f32[16,8,4096]{2,1,0:T(8,128)}, u32[]{:S(2)}, u32[]{:S(2)}) async-start(f32[16,8,4096]{2,1,0:T(8,128)} %shard_map.85), calls=%async_computation.2 | async-start | bytes 4194304 | tf_op jit(solution)/shard_map/all_to_all | solution.py:259
  114.3 52.4 %all-to-all-start.4 = ((f32[16,8,4096]{2,1,0:T(8,128)}), f32[16,8,4096]{2,1,0:T(8,128)}, u32[]{:S(2)}, u32[]{:S(2)}) async-start(f32[16,8,4096]{2,1,0:T(8,128)} %shard_map.87), calls=%async_computation.4 | async-start | bytes 4194304 | tf_op jit(solution)/shard_map/all_to_all | solution.py:259
  126.2 45.4 %copy-start.6 = (f32[7]{0:T(128)S(1)}, f32[7]{0:T(128)}, u32[]{:S(2)}) copy-start(f32[7]{0:T(128)} %param.16) | copy-start | bytes 88
  126.2 45.4 %copy-start.8 = (f32[7]{0:T(128)S(1)}, f32[7]{0:T(128)}, u32[]{:S(2)}) copy-start(f32[7]{0:T(128)} %constant.123.clone) | copy-start | bytes 88
  126.2 45.4 %copy-start.7 = (s32[128]{0:T(128)S(1)}, s32[128]{0:T(128)}, u32[]{:S(2)}) copy-start(s32[128]{0:T(128)} %param.19) | copy-start | bytes 1540
  166.7 52.3 %all-to-all-start.6 = ((f32[16,8,4096]{2,1,0:T(8,128)}), f32[16,8,4096]{2,1,0:T(8,128)S(1)}, u32[]{:S(2)}, u32[]{:S(2)}) async-start(f32[16,8,4096]{2,1,0:T(8,128)} %shard_map.89), calls=%async_computation.6 | async-start | bytes 4194304 | tf_op jit(solution)/shard_map/all_to_all | solution.py:259
  219.0 1.4 copy-start.2
  220.4 52.3 %all-to-all-start.1 = ((f32[16,8,4096]{2,1,0:T(8,128)}), f32[16,8,4096]{2,1,0:T(8,128)S(1)}, u32[]{:S(2)}, u32[]{:S(2)}) async-start(f32[16,8,4096]{2,1,0:T(8,128)} %fusion.7), calls=%async_computation.1 | async-start | bytes 4194304 | tf_op jit(solution)/shard_map/all_to_all | solution.py:301
  272.7 52.4 %all-to-all-start.3 = ((f32[16,8,4096]{2,1,0:T(8,128)}), f32[16,8,4096]{2,1,0:T(8,128)}, u32[]{:S(2)}, u32[]{:S(2)}) async-start(f32[16,8,4096]{2,1,0:T(8,128)} %fusion.5), calls=%async_computation.3 | async-start | bytes 4194304 | tf_op jit(solution)/shard_map/all_to_all | solution.py:301
  325.2 52.4 %all-to-all-start.5 = ((f32[16,8,4096]{2,1,0:T(8,128)}), f32[16,8,4096]{2,1,0:T(8,128)}, u32[]{:S(2)}, u32[]{:S(2)}) async-start(f32[16,8,4096]{2,1,0:T(8,128)} %fusion.3), calls=%async_computation.5 | async-start | bytes 4194304 | tf_op jit(solution)/shard_map/all_to_all | solution.py:301
  330.1 9.1 %copy-start.4 = (s32[8]{0:T(128)S(1)}, s32[8]{0:T(128)}, u32[]{:S(2)}) copy-start(s32[8]{0:T(128)} %param.20) | copy-start | bytes 100
  330.1 9.2 %copy-start.3 = (f32[16,8,4096]{2,1,0:T(8,128)S(1)}, f32[16,8,4096]{2,1,0:T(8,128)}, u32[]{:S(2)}) copy-start(f32[16,8,4096]{2,1,0:T(8,128)} %copy-done.2) | copy-start | bytes 6291460
  377.6 111.6 %all-to-all-start.7 = ((f32[16,8,4096]{2,1,0:T(8,128)}), f32[16,8,4096]{2,1,0:T(8,128)}, u32[]{:S(2)}, u32[]{:S(2)}) async-start(f32[16,8,4096]{2,1,0:T(8,128)} %fusion.1), calls=%async_computation.7 | async-start | bytes 4194304 | tf_op jit(solution)/shard_map/all_to_all | solution.py:301
  382.5 6.7 %copy-start.5 = (s32[1024]{0:T(1024)S(1)}, s32[1024]{0:T(1024)}, u32[]{:S(2)}) copy-start(s32[1024]{0:T(1024)} %param.18) | copy-start | bytes 12292
  386.9 54.2 %collective-permute-start = (f32[4,65536]{1,0:T(4,128)}, f32[4,65536]{1,0:T(4,128)S(1)}, u32[]{:S(2)}, u32[]{:S(2)}) collective-permute-start(f32[4,65536]{1,0:T(4,128)} %fusion.14), channel_id=1, source_target_pairs={{1,0},{2,1},{3,2},{4,3},{5,4},{6,5},{7,6},{8,7},{9,8},{10,9},{11,1... | collective-permute-start | bytes 3145736 | tf_op jit(solution)/shard_map/ppermute | solution.py:21
  489.2 6.9 %copy-start.1 = (f32[16]{0:T(128)S(1)}, f32[16]{0:T(128)}, u32[]{:S(2)}) copy-start(f32[16]{0:T(128)} %param.17) | copy-start | bytes 196

commit v2 on v1

--- a/solution.py
+++ b/solution.py
@@ -42,32 +42,35 @@
     return jnp.dot(single_selector, unlocking_coefficients_by_grade, precision=HIGHEST)
 
 
-def on_state(start, velocity, bound, component, blocks):
+def on_state(start, velocity, bound_cells, pair, blocks):
     _, _, rows, cells = start.shape
     width = cells // blocks
     per_step = max(1, min(blocks, 8192 // width))
-    planes = width // P2 if width >= P2 else 1
 
     def kernel(bound_ref, start_ref, velocity_ref, out_ref):
         step = pl.program_id(0)
-        value = start_ref[...] + section_step * velocity_ref[...]
-        cell = step * (per_step * width) + lax.broadcasted_iota(jnp.int32, value.shape, 1)
-        value = jnp.where((cell // P2) < bound_ref[:, 0:1], value, 0.0)
+        lane = lax.broadcasted_iota(jnp.int32, (rows, width), 1)
         for part in range(per_step):
-            out_ref[part] = value[:, part * width : (part + 1) * width]
-
-    spec = pl.BlockSpec((None, None, rows, per_step * width), lambda j: (component, 1, 0, j))
+            lanes = slice(part * width, (part + 1) * width)
+            limit = bound_ref[:, 0:1] - (step * per_step + part) * width
+            for comp in range(2):
+                value = start_ref[comp, :, lanes] + section_step * velocity_ref[comp, :, lanes]
+                out_ref[part, :, comp * width : (comp + 1) * width] = jnp.where(
+                    lane < limit, value, 0.0
+                )
+
+    spec = pl.BlockSpec((2, None, rows, per_step * width), lambda j: (pair, 1, 0, j))
     return pl.pallas_call(
         kernel,
         grid=(blocks // per_step,),
         in_specs=[pl.BlockSpec((rows, 128), lambda j: (0, 0)), spec, spec],
-        out_specs=pl.BlockSpec((per_step, rows, width), lambda j: (j, 0, 0)),
-        out_shape=jax.ShapeDtypeStruct((blocks, rows, width), jnp.float32),
+        out_specs=pl.BlockSpec((per_step, rows, 2 * width), lambda j: (j, 0, 0)),
+        out_shape=jax.ShapeDtypeStruct((blocks, rows, 2 * width), jnp.float32),
         compiler_params=pltpu.CompilerParams(vmem_limit_bytes=VMEM_LIMIT),
         cost_estimate=pl.CostEstimate(
-            flops=3 * rows * cells, bytes_accessed=12 * rows * cells, transcendentals=0
+            flops=6 * rows * cells, bytes_accessed=24 * rows * cells, transcendentals=0
         ),
-    )(bound, start, velocity)
+    )(bound_cells, start, velocity)
 
 
 def partial_slope(start, velocity, halo, rates, bound, row_rates, diagonals, columns):
@@ -199,39 +202,41 @@
     )(rates, bound, row_rates, diagonals, columns, start, velocity, start, velocity, start, velocity, halo)
 
 
-def add_rows(slope, returned, bound, component):
+def add_rows(slope, returned, bound_cells, pair):
     _, _, rows, cells = slope.shape
-    blocks, _, width = returned.shape
+    blocks = returned.shape[0]
+    width = cells // blocks
     per_step = max(1, min(blocks, 8192 // width))
 
     def kernel(bound_ref, slope_ref, returned_ref, out_ref):
         step = pl.program_id(0)
+        lane = lax.broadcasted_iota(jnp.int32, (rows, width), 1)
         for part in range(per_step):
-            cell = (step * per_step + part) * width + lax.broadcasted_iota(
-                jnp.int32, (rows, width), 1
-            )
             lanes = slice(part * width, (part + 1) * width)
-            out_ref[:, lanes] = slope_ref[:, lanes] + jnp.where(
-                (cell // P2) < bound_ref[:, 0:1], returned_ref[part], 0.0
-            )
-
-    spec = pl.BlockSpec((None, None, rows, per_step * width), lambda j: (component, 1, 0, j))
+            limit = bound_ref[:, 0:1] - (step * per_step + part) * width
+            for comp in range(2):
+                value = returned_ref[part, :, comp * width : (comp + 1) * width]
+                out_ref[comp, :, lanes] = slope_ref[comp, :, lanes] + jnp.where(
+                    lane < limit, value, 0.0
+                )
+
+    spec = pl.BlockSpec((2, None, rows, per_step * width), lambda j: (pair, 1, 0, j))
     return pl.pallas_call(
         kernel,
         grid=(blocks // per_step,),
         in_specs=[
             pl.BlockSpec((rows, 128), lambda j: (0, 0)),
             spec,
-            pl.BlockSpec((per_step, rows, width), lambda j: (j, 0, 0)),
+            pl.BlockSpec((per_step, rows, 2 * width), lambda j: (j, 0, 0)),
         ],
         out_specs=spec,
         out_shape=jax.ShapeDtypeStruct(slope.shape, jnp.float32),
         input_output_aliases={1: 0},
         compiler_params=pltpu.CompilerParams(vmem_limit_bytes=VMEM_LIMIT),
         cost_estimate=pl.CostEstimate(
-            flops=2 * rows * cells, bytes_accessed=12 * rows * cells, transcendentals=0
+            flops=4 * rows * cells, bytes_accessed=24 * rows * cells, transcendentals=0
         ),
-    )(bound, slope, returned)
+    )(bound_cells, slope, returned)
 
 
 def local(
@@ -252,17 +257,21 @@
     burst, trans, off, mdecay, decay1, make2, decay2 = [rates[place] for place in range(7)]
     bound = jnp.broadcast_to(upper_bounds_per_abundance[:, None], (rows, 128))
 
-    order = (2, 3, 0, 1)
-    arrived = {}
-    for comp in order:
-        sent = on_state(start, velocity, bound, comp, blocks)
-        came = lax.all_to_all(sent, "slab", split_axis=0, concat_axis=0, tiled=True)
-        arrived[comp] = came.reshape(breadth, width)
+    bound_cells = bound * P2
+
+    def exchanged(value):
+        return lax.all_to_all(value, "slab", split_axis=0, concat_axis=0, tiled=True)
 
     first_index = jnp.arange(cells, dtype=jnp.int32) // P2
     lowest = start[:, 0, 0, :] + section_step * velocity[:, 0, 0, :]
     lowest = jnp.where(first_index[None, :] < upper_bounds_per_abundance[0], lowest, 0.0)
     halo = shifted(lowest, "slab", -1)
+
+    came_late = exchanged(on_state(start, velocity, bound_cells, 1, blocks))
+    sent_early, halo = lax.optimization_barrier(
+        (on_state(start, velocity, bound_cells, 0, blocks), halo)
+    )
+    came_early = exchanged(sent_early)
 
     first_row = lax.axis_index("slab") * rows
     m_count = (first_row + jnp.arange(rows, dtype=jnp.int32)).astype(jnp.float32)
@@ -293,17 +302,15 @@
     )
     matrix = episodes + removal
 
-    returned = {}
-    for comp in order:
-        total = jnp.dot(matrix, arrived[comp], precision=HIGHEST)
-        if comp == 1:
-            total = total + jnp.dot(episodes, arrived[0], precision=HIGHEST)
-        returned[comp] = lax.all_to_all(
-            total.reshape(blocks, rows, width), "slab", split_axis=0, concat_axis=0, tiled=True
-        )
-    for comp in order:
-        slope = add_rows(slope, returned[comp], bound, comp)
-    return slope
+    total_late = jnp.dot(matrix, came_late.reshape(breadth, 2 * width), precision=HIGHEST)
+    total_late, slope = lax.optimization_barrier((total_late, slope))
+    returned_late = exchanged(total_late.reshape(blocks, rows, 2 * width))
+    fields = came_early.reshape(breadth, 2 * width)
+    source = jnp.dot(episodes, fields[:, :width], precision=HIGHEST)
+    total_early = jnp.dot(matrix, fields, precision=HIGHEST) + jnp.pad(source, ((0, 0), (width, 0)))
+    returned_early = exchanged(total_early.reshape(blocks, rows, 2 * width))
+    slope = add_rows(slope, returned_late, bound_cells, 1)
+    return add_rows(slope, returned_early, bound_cells, 0)
 
 
 def solution(mesh):

time: 498 us -> 419 us (0.84)
  Pallas kernels: 83 us -> 55.4 us
  waiting for transfers between devices: 315 us -> 291 us
  starting transfers between devices: 43.2 us -> 23.1 us
  matrix products: 34.2 us -> 29 us
    all_to_all x8 -> x4, waiting for transfers between devices: 267 us -> 207 us  [exchanged(): lax.all_to_all(value, 'slab', split_axis=0, concat_axis=0, tiled=True)]
    ppermute x1, waiting for transfers between devices: 47.8 us -> 84 us  [shifted(): lax.ppermute(value, axis, [(source, source + steps) for source in range(f...]
    all_to_all x8 -> x4, starting transfers between devices: 40.9 us -> 20.8 us  [exchanged(): lax.all_to_all(value, 'slab', split_axis=0, concat_axis=0, tiled=True)]
    pallas_call x4 -> x2, Pallas kernels: 28.1 us -> 11.8 us  [on_state(): pl.pallas_call(kernel, grid=(blocks // per_step,), in_specs=[pl.BlockSpec...]
    pallas_call x4 -> x2, Pallas kernels: 27.1 us -> 15.8 us  [add_rows(): pl.pallas_call(kernel, grid=(blocks // per_step,), in_specs=[pl.BlockSpec...]
    dot_general x5 -> x3, matrix products: 27.3 us -> 22 us  [the longest x1 9.06 us: local(): jnp.dot(matrix, fields, precision=HIGHEST)]
  transfers between devices with their start and end apart: 9 -> 5, of which waited for: 8 -> 4; matrix products, arithmetic and copies ran while one was open for 11% -> 10% of each run, Pallas kernels for 14% -> 10%
where the time goes in v2:
time: 419 us; the launch traced here: 418 us
  waiting for transfers between devices  291 us (69%)
  Pallas kernels  55.4 us (13%)
  matrix products  29 us (7%)
  starting transfers between devices  23.1 us (6%)
  local copies, waits for them, and re-layouts  13 us (3%)
  other arithmetic  6.1 us (1%)
    all_to_all x4, waiting for transfers between devices, exchanged(): lax.all_to_all(value, 'slab', split_axis=0, concat_axis=0, tiled=True)  207 us
    ppermute x1, waiting for transfers between devices, shifted(): lax.ppermute(value, axis, [(source, source + steps) for source in range(f...  84 us
    pallas_call x1, Pallas kernels, partial_slope(): pl.pallas_call(kernel, grid=(steps,), in_specs=[pl.BlockSpec(memory_space...  27.8 us
    all_to_all x4, starting transfers between devices, exchanged(): lax.all_to_all(value, 'slab', split_axis=0, concat_axis=0, tiled=True)  20.8 us
    pallas_call x2, Pallas kernels, add_rows(): pl.pallas_call(kernel, grid=(blocks // per_step,), in_specs=[pl.BlockSpec...  15.8 us
    pallas_call x2, Pallas kernels, on_state(): pl.pallas_call(kernel, grid=(blocks // per_step,), in_specs=[pl.BlockSpec...  11.8 us
    dot_general x1, matrix products, local(): jnp.dot(matrix, fields, precision=HIGHEST)  9.06 us
    dot_general x1, matrix products, local(): jnp.dot(matrix, came_late.reshape(breadth, 2 * width), precision=HIGHEST)  8.95 us
  transfers between devices with their start and end apart: 5, of which 4 were waited for; matrix products, arithmetic and copies ran while one was open for 10% of the time, Pallas kernels for 10%

profile of v2, /device:TPU:11, one launch (start us, length us, event | category | flops | bytes accessed | tf_op | source)
XLA Modules:
  0.0 417.9 jit_solution(12549041768112749040)
XLA Ops:
  0.0 0.7 broadcast_multiply_fusion
  0.7 5.9 %shard_map.82 = f32[16,8,8192]{2,1,0:T(8,128)S(1)} custom-call(s32[8,128]{1,0:T(8,128)S(1)} %broadcast_in_dim.21.bound_ref, f32[4,2,8,65536]{3,2,1,0:T(8,128)} %start_high.1, f32[4,2,8,65536]{3,2,1,0:T(8,128)} %velocity_high.1), custom_call_target="tpu_custom_call" | custom-call | flops 3145728 | bytes 12582912 | tf_op jit(solution)/shard_map/pallas_call | solution.py:63
  6.6 2.0 copy-done.3
  8.6 6.6 %all-to-all-start = ((f32[16,8,8192]{2,1,0:T(8,128)}), f32[16,8,8192]{2,1,0:T(8,128)}, u32[]{:S(2)}, u32[]{:S(2)}) async-start(f32[16,8,8192]{2,1,0:T(8,128)} %copy-done.3), calls=%async_computation | async-start | bytes 8388608 | tf_op jit(solution)/shard_map/all_to_all | solution.py:263
  15.2 3.9 slice.77
  19.1 3.9 slice.78
  23.2 1.4 fusion.9
  24.6 2.3 collective-permute-start
  26.9 5.9 %shard_map.83 = f32[16,8,8192]{2,1,0:T(8,128)S(1)} custom-call(s32[8,128]{1,0:T(8,128)S(1)} %broadcast_in_dim.21.bound_ref, f32[4,2,8,65536]{3,2,1,0:T(8,128)} %start_high.1, f32[4,2,8,65536]{3,2,1,0:T(8,128)} %velocity_high.1), custom_call_target="tpu_custom_call" | custom-call | flops 3145728 | bytes 12582912 | tf_op jit(solution)/shard_map/pallas_call | solution.py:63
  32.8 2.0 copy-done.2
  34.7 84.0 %collective-permute-done.halo_ref = f32[4,65536]{1,0:T(4,128)S(1)} collective-permute-done((f32[4,65536]{1,0:T(4,128)S(1)}, f32[4,65536]{1,0:T(4,128)S(1)}, u32[]{:S(2)}, u32[]{:S(2)}) %collective-permute-start) | collective-permute-done | bytes 1048608 | tf_op jit(solution)/shard_map/ppermute | solution.py:21
  118.8 4.5 %all-to-all-start.2 = ((f32[16,8,8192]{2,1,0:T(8,128)}), f32[16,8,8192]{2,1,0:T(8,128)}, u32[]{:S(2)}, u32[]{:S(2)}) async-start(f32[16,8,8192]{2,1,0:T(8,128)} %copy-done.2), calls=%async_computation.2 | async-start | bytes 8388608 | tf_op jit(solution)/shard_map/all_to_all | solution.py:263
  123.3 0.4 fusion.10
  123.9 0.7 fusion.26
  124.6 0.7 compare_select_fusion
  125.4 0.7 convert_multiply_fusion.1
  126.1 0.6 add_multiply_fusion
  126.7 0.7 iota_multiply_fusion
  127.3 0.6 fusion.22
  128.1 0.7 subtract_subtract_fusion
  128.8 6.5 %fusion.1 = f32[1,128,128]{2,0,1:T(1,128)S(1)} fusion(s32[128,128]{1,0:T(8,128)S(1)} %iota_subtract_fusion, f32[]{:T(128)} %fusion.22, s32[128]{0:T(128)S(1)} %copy-done.7), kind=kOutput, calls=%fused_computation.3 | convolution fusion | flops 27263488 | bytes 131588 | tf_op jit(solution)/shard_map/dot_general | solution.py:34
  135.3 27.8 %shard_map.84.slope_ref = f32[4,2,8,65536]{3,2,1,0:T(8,128)} custom-call(f32[7]{0:T(128)S(1)} %mul.103.rate_ref, s32[8,128]{1,0:T(8,128)S(1)} %broadcast_in_dim.22.bound_ref, f32[8,256]{1,0:T(8,128)S(1)} %pad_maximum_fusion.1.row_ref, f32[2,8,1024]{2,1,0:T(8,128)S(1)} %pad_maximum_fusion.diagonal_ref, f32[8,1024]{1,0:T(8,128)S(1)} %scatter.14.column_ref, ...), custom_call_target="tpu_custom_call" | custom-call | flops 125829120 | bytes 67108864 | tf_op jit(solution)/shard_map/pallas_call | solution.py:178
  163.2 9.0 %fusion.2 = f32[128,8192]{1,0:T(8,128)} fusion(f32[16,8,8192]{2,1,0:T(8,128)} %all-to-all-done, f32[128,128]{1,0:T(8,128)S(1)} %bitcast.30, f32[128]{0:T(128)S(1)} %iota_add_fusion.1, s32[128]{0:T(128)S(1)} %iota_add_fusion.2, f32[]{:T(128)} %bitcast.4, f32[]{:T(128)} %bitcast), kind=kOutput, calls=%fused_computation.4 | convolution fusion | flops 1610776576 | bytes 8455176 | tf_op jit(solution)/shard_map/dot_general | solution.py:305
  172.1 43.1 %all-to-all-done.2 = f32[16,8,8192]{2,1,0:T(8,128)} async-done(((f32[16,8,8192]{2,1,0:T(8,128)}), f32[16,8,8192]{2,1,0:T(8,128)}, u32[]{:S(2)}, u32[]{:S(2)}) %all-to-all-start.2) | async-done | bytes 4194336 | tf_op jit(solution)/shard_map/all_to_all | solution.py:263
  215.2 4.9 %all-to-all-start.1 = ((f32[16,8,8192]{2,1,0:T(8,128)}), f32[16,8,8192]{2,1,0:T(8,128)}, u32[]{:S(2)}, u32[]{:S(2)}) async-start(f32[16,8,8192]{2,1,0:T(8,128)} %bitcast.29), calls=%async_computation.1 | async-start | bytes 8388608 | tf_op jit(solution)/shard_map/all_to_all | solution.py:263
  220.1 4.0 fusion.5
  224.2 9.1 %fusion = f32[16,8,8192]{2,1,0:T(8,128)} fusion(f32[128,4096]{1,0:T(8,128)S(1)} %fusion.5, f32[16,8,8192]{2,1,0:T(8,128)} %all-to-all-done.2, f32[128,128]{1,0:T(8,128)S(1)} %bitcast.32, f32[128]{0:T(128)S(1)} %iota_add_fusion.1, s32[128]{0:T(128)S(1)} %iota_add_fusion.2, f32[]{:T(128)} %bitcast.4, f32[]{:T(128)} %bitcast), kind=kOutput, calls=%fused_computation.1 | convolution fusion | flops 1611825152 | bytes 10552328 | tf_op jit(solution)/shard_map/dot_general | solution.py:310
  233.2 79.4 %all-to-all-done.1.returned_ref = f32[16,8,8192]{2,1,0:T(8,128)} async-done(((f32[16,8,8192]{2,1,0:T(8,128)}), f32[16,8,8192]{2,1,0:T(8,128)}, u32[]{:S(2)}, u32[]{:S(2)}) %all-to-all-start.1) | async-done | bytes 4194336 | tf_op jit(solution)/shard_map/all_to_all | solution.py:263
  312.6 4.9 %all-to-all-start.3 = ((f32[16,8,8192]{2,1,0:T(8,128)}), f32[16,8,8192]{2,1,0:T(8,128)}, u32[]{:S(2)}, u32[]{:S(2)}) async-start(f32[16,8,8192]{2,1,0:T(8,128)} %fusion), calls=%async_computation.3 | async-start | bytes 8388608 | tf_op jit(solution)/shard_map/all_to_all | solution.py:263
  317.5 7.9 %shard_map.85.slope_ref = f32[4,2,8,65536]{3,2,1,0:T(8,128)} custom-call(s32[8,128]{1,0:T(8,128)S(1)} %broadcast_in_dim.21.bound_ref, f32[4,2,8,65536]{3,2,1,0:T(8,128)} %shard_map.84.slope_ref, f32[16,8,8192]{2,1,0:T(8,128)} %all-to-all-done.1.returned_ref), custom_call_target="tpu_custom_call", output_to_operand_aliasing={{}: (1, {})} | custom-call | flops 2097152 | bytes 12582912 | tf_op jit(solution)/shard_map/pallas_call | solution.py:224
  325.4 84.6 %all-to-all-done.3.returned_ref = f32[16,8,8192]{2,1,0:T(8,128)} async-done(((f32[16,8,8192]{2,1,0:T(8,128)}), f32[16,8,8192]{2,1,0:T(8,128)}, u32[]{:S(2)}, u32[]{:S(2)}) %all-to-all-start.3) | async-done | bytes 4194336 | tf_op jit(solution)/shard_map/all_to_all | solution.py:263
  410.0 7.9 %shard_map.86 = f32[4,2,8,65536]{3,2,1,0:T(8,128)} custom-call(s32[8,128]{1,0:T(8,128)S(1)} %broadcast_in_dim.21.bound_ref, f32[4,2,8,65536]{3,2,1,0:T(8,128)} %shard_map.85.slope_ref, f32[16,8,8192]{2,1,0:T(8,128)} %all-to-all-done.3.returned_ref), custom_call_target="tpu_custom_call", output_to_operand_aliasing={{}: (1, {})} | custom-call | flops 2097152 | bytes 12582912 | tf_op jit(solution)/shard_map/pallas_call | solution.py:224
  (32 shorter events, 0.7 us)
Async XLA Ops:
  0.0 123.3 %copy-start = (f32[16]{0:T(128)S(1)}, f32[16]{0:T(128)}, u32[]{:S(2)}) copy-start(f32[16]{0:T(128)} %param.17) | copy-start | bytes 196
  6.6 2.0 copy-start.3
  8.6 110.2 %all-to-all-start = ((f32[16,8,8192]{2,1,0:T(8,128)}), f32[16,8,8192]{2,1,0:T(8,128)}, u32[]{:S(2)}, u32[]{:S(2)}) async-start(f32[16,8,8192]{2,1,0:T(8,128)} %copy-done.3), calls=%async_computation | async-start | bytes 8388608 | tf_op jit(solution)/shard_map/all_to_all | solution.py:263
  15.2 7.9 %copy-start.4 = (s32[8]{0:T(128)S(1)}, s32[8]{0:T(128)}, u32[]{:S(2)}) copy-start(s32[8]{0:T(128)} %param.20) | copy-start | bytes 100
  24.6 94.2 %collective-permute-start = (f32[4,65536]{1,0:T(4,128)S(1)}, f32[4,65536]{1,0:T(4,128)S(1)}, u32[]{:S(2)}, u32[]{:S(2)}) collective-permute-start(f32[4,65536]{1,0:T(4,128)S(1)} %fusion.9), channel_id=1, source_target_pairs={{1,0},{2,1},{3,2},{4,3},{5,4},{6,5},{7,6},{8,7},{9,8},{10,9},{11,1... | collective-permute-start | bytes 3145736 | tf_op jit(solution)/shard_map/ppermute | solution.py:21
  32.8 2.0 copy-start.2
  34.7 88.5 %copy-start.6 = (f32[7]{0:T(128)S(1)}, f32[7]{0:T(128)}, u32[]{:S(2)}) copy-start(f32[7]{0:T(128)} %param.16) | copy-start | bytes 88
  34.7 88.5 %copy-start.8 = (f32[7]{0:T(128)S(1)}, f32[7]{0:T(128)}, u32[]{:S(2)}) copy-start(f32[7]{0:T(128)} %constant.127.clone) | copy-start | bytes 88
  34.7 88.6 %copy-start.5 = (s32[1024]{0:T(1024)S(1)}, s32[1024]{0:T(1024)}, u32[]{:S(2)}) copy-start(s32[1024]{0:T(1024)} %param.18) | copy-start | bytes 12292
  34.7 92.6 %copy-start.7 = (s32[128]{0:T(128)S(1)}, s32[128]{0:T(128)}, u32[]{:S(2)}) copy-start(s32[128]{0:T(128)} %param.19) | copy-start | bytes 1540
  118.8 96.4 %all-to-all-start.2 = ((f32[16,8,8192]{2,1,0:T(8,128)}), f32[16,8,8192]{2,1,0:T(8,128)}, u32[]{:S(2)}, u32[]{:S(2)}) async-start(f32[16,8,8192]{2,1,0:T(8,128)} %copy-done.2), calls=%async_computation.2 | async-start | bytes 8388608 | tf_op jit(solution)/shard_map/all_to_all | solution.py:263
  215.2 97.4 %all-to-all-start.1 = ((f32[16,8,8192]{2,1,0:T(8,128)}), f32[16,8,8192]{2,1,0:T(8,128)}, u32[]{:S(2)}, u32[]{:S(2)}) async-start(f32[16,8,8192]{2,1,0:T(8,128)} %bitcast.29), calls=%async_computation.1 | async-start | bytes 8388608 | tf_op jit(solution)/shard_map/all_to_all | solution.py:263
  312.6 97.4 %all-to-all-start.3 = ((f32[16,8,8192]{2,1,0:T(8,128)}), f32[16,8,8192]{2,1,0:T(8,128)}, u32[]{:S(2)}, u32[]{:S(2)}) async-start(f32[16,8,8192]{2,1,0:T(8,128)} %fusion), calls=%async_computation.3 | async-start | bytes 8388608 | tf_op jit(solution)/shard_map/all_to_all | solution.py:263
  410.0 7.9 %copy-start.1 = (f32[16]{0:T(128)S(1)}, f32[16]{0:T(128)}, u32[]{:S(2)}) copy-start(f32[16]{0:T(128)} %param.17) | copy-start | bytes 196

commit v3 on v2

--- a/solution.py
+++ b/solution.py
@@ -239,6 +239,134 @@
     )(bound_cells, slope, returned)
 
 
+def exchange_rest(matrix, episodes, came_late, sent_early, rows):
+    blocks, _, wide = sent_early.shape
+    breadth = blocks * rows
+    half = wide // 2
+    tile = min(512, half)
+
+    def kernel(
+        matrix_ref,
+        episode_ref,
+        late_ref,
+        sent_ref,
+        late_out,
+        early_out,
+        fields,
+        late_total,
+        early_total,
+        send_sem,
+        recv_sem,
+        own_sem,
+    ):
+        me = lax.axis_index("slab")
+        barrier = pltpu.get_barrier_semaphore()
+
+        @pl.loop(1, blocks)
+        def _(hop):
+            pl.semaphore_signal(
+                barrier,
+                inc=1,
+                device_id={"slab": lax.rem(me + hop, blocks)},
+                device_id_type=pl.DeviceIdType.MESH,
+            )
+
+        pl.semaphore_wait(barrier, blocks - 1)
+
+        def transfer(phase, source, target, hop):
+            peer = lax.rem(me + hop, blocks)
+            return pltpu.make_async_remote_copy(
+                src_ref=source.at[peer],
+                dst_ref=target.at[me],
+                send_sem=send_sem.at[phase, hop],
+                recv_sem=recv_sem.at[phase, hop],
+                device_id={"slab": peer},
+                device_id_type=pl.DeviceIdType.MESH,
+            )
+
+        def start(phase, source, target):
+            @pl.loop(1, blocks)
+            def _(hop):
+                transfer(phase, source, target, hop).start()
+
+            pltpu.make_async_copy(source.at[me], target.at[me], own_sem.at[phase]).start()
+
+        def arrive(phase, source, target):
+            @pl.loop(1, blocks)
+            def _(hop):
+                transfer(phase, source, target, hop).wait_recv()
+
+            pltpu.make_async_copy(source.at[me], target.at[me], own_sem.at[phase]).wait()
+
+        def leave(phase, source, target):
+            @pl.loop(1, blocks)
+            def _(hop):
+                transfer(phase, source, target, hop).wait_send()
+
+        start(0, sent_ref, fields)
+
+        def product(left, right):
+            return jnp.dot(
+                left, right.reshape(breadth, tile), precision=HIGHEST,
+                preferred_element_type=jnp.float32,
+            )
+
+        @pl.loop(0, wide // tile)
+        def _(step):
+            lanes = pl.ds(pl.multiple_of(step * tile, tile), tile)
+            total = product(matrix_ref[...], late_ref[:, :, lanes])
+            late_total[:, :, lanes] = total.reshape(blocks, rows, tile)
+
+        start(1, late_total, late_out)
+        arrive(0, sent_ref, fields)
+
+        @pl.loop(0, half // tile)
+        def _(step):
+            lanes = pl.ds(pl.multiple_of(step * tile, tile), tile)
+            beyond = pl.ds(pl.multiple_of(half + step * tile, tile), tile)
+            first = fields[:, :, lanes]
+            total = product(matrix_ref[...], first)
+            early_total[:, :, lanes] = total.reshape(blocks, rows, tile)
+            total = product(matrix_ref[...], fields[:, :, beyond]) + product(
+                episode_ref[...], first
+            )
+            early_total[:, :, beyond] = total.reshape(blocks, rows, tile)
+
+        start(2, early_total, early_out)
+        arrive(1, late_total, late_out)
+        arrive(2, early_total, early_out)
+        leave(0, sent_ref, fields)
+        leave(1, late_total, late_out)
+        leave(2, early_total, early_out)
+
+    shape = jax.ShapeDtypeStruct(sent_early.shape, jnp.float32)
+    vmem = pl.BlockSpec(memory_space=pltpu.VMEM)
+    anywhere = pl.BlockSpec(memory_space=pl.ANY)
+    buffer = pltpu.VMEM(sent_early.shape, jnp.float32)
+    return pl.pallas_call(
+        kernel,
+        in_specs=[vmem, vmem, vmem, anywhere],
+        out_specs=[anywhere, anywhere],
+        out_shape=[shape, shape],
+        scratch_shapes=[
+            buffer,
+            buffer,
+            buffer,
+            pltpu.SemaphoreType.DMA((3, blocks)),
+            pltpu.SemaphoreType.DMA((3, blocks)),
+            pltpu.SemaphoreType.DMA((3,)),
+        ],
+        compiler_params=pltpu.CompilerParams(
+            collective_id=0, has_side_effects=True, vmem_limit_bytes=VMEM_LIMIT
+        ),
+        cost_estimate=pl.CostEstimate(
+            flops=6 * breadth * breadth * wide,
+            bytes_accessed=24 * breadth * wide,
+            transcendentals=0,
+        ),
+    )(matrix, episodes, came_late, sent_early)
+
+
 def local(
     starting_joint_sensitivities,
     former_section_velocity,
@@ -268,10 +396,7 @@
     halo = shifted(lowest, "slab", -1)
 
     came_late = exchanged(on_state(start, velocity, bound_cells, 1, blocks))
-    sent_early, halo = lax.optimization_barrier(
-        (on_state(start, velocity, bound_cells, 0, blocks), halo)
-    )
-    came_early = exchanged(sent_early)
+    sent_early = on_state(start, velocity, bound_cells, 0, blocks)
 
     first_row = lax.axis_index("slab") * rows
     m_count = (first_row + jnp.arange(rows, dtype=jnp.int32)).astype(jnp.float32)
@@ -302,13 +427,8 @@
     )
     matrix = episodes + removal
 
-    total_late = jnp.dot(matrix, came_late.reshape(breadth, 2 * width), precision=HIGHEST)
-    total_late, slope = lax.optimization_barrier((total_late, slope))
-    returned_late = exchanged(total_late.reshape(blocks, rows, 2 * width))
-    fields = came_early.reshape(breadth, 2 * width)
-    source = jnp.dot(episodes, fields[:, :width], precision=HIGHEST)
-    total_early = jnp.dot(matrix, fields, precision=HIGHEST) + jnp.pad(source, ((0, 0), (width, 0)))
-    returned_early = exchanged(total_early.reshape(blocks, rows, 2 * width))
+    came_late, sent_early, slope = lax.optimization_barrier((came_late, sent_early, slope))
+    returned_late, returned_early = exchange_rest(matrix, episodes, came_late, sent_early, rows)
     slope = add_rows(slope, returned_late, bound_cells, 1)
     return add_rows(slope, returned_early, bound_cells, 0)
 

time: 419 us -> 439 us (1.048)
  Pallas kernels: 55.4 us -> 331 us
  waiting for transfers between devices: 291 us -> 70.6 us
  matrix products: 29 us -> 6.96 us
  starting transfers between devices: 23.1 us -> 8.97 us
    pallas_call x0 -> x1, Pallas kernels: none -> 277 us  [exchange_rest(): pl.pallas_call(kernel, in_specs=[vmem, vmem, vmem, anywhere], out_specs=[...]
    all_to_all x4 -> x1, waiting for transfers between devices: 207 us -> 0.01 us  [exchanged(): lax.all_to_all(value, 'slab', split_axis=0, concat_axis=0, tiled=True)]
    dot_general x3 -> x0, matrix products: 22 us -> none  [the longest x1 9.06 us: local(): jnp.dot(matrix, fields, precision=HIGHEST)]
    all_to_all x4 -> x1, starting transfers between devices: 20.8 us -> 6.7 us  [exchanged(): lax.all_to_all(value, 'slab', split_axis=0, concat_axis=0, tiled=True)]
    ppermute x1, waiting for transfers between devices: 84 us -> 70.6 us  [shifted(): lax.ppermute(value, axis, [(source, source + steps) for source in range(f...]
  transfers between devices with their start and end apart: 5 -> 2, of which waited for: 4 -> 1; matrix products, arithmetic and copies ran while one was open for 10% -> 5% of each run, Pallas kernels for 10% -> 8%
where the time goes in v3:
time: 439 us
  Pallas kernels  331 us (75%)
  waiting for transfers between devices  70.6 us (16%)
  local copies, waits for them, and re-layouts  13 us (3%)
  starting transfers between devices  8.97 us (2%)
  other arithmetic  7.58 us (2%)
  matrix products  6.96 us (2%)
    pallas_call x1, Pallas kernels, exchange_rest(): pl.pallas_call(kernel, in_specs=[vmem, vmem, vmem, anywhere], out_specs=[...  277 us
    ppermute x1, waiting for transfers between devices, shifted(): lax.ppermute(value, axis, [(source, source + steps) for source in range(f...  70.6 us
    pallas_call x1, Pallas kernels, partial_slope(): pl.pallas_call(kernel, grid=(steps,), in_specs=[pl.BlockSpec(memory_space...  28 us
    pallas_call x2, Pallas kernels, add_rows(): pl.pallas_call(kernel, grid=(blocks // per_step,), in_specs=[pl.BlockSpec...  14.6 us
    pallas_call x2, Pallas kernels, on_state(): pl.pallas_call(kernel, grid=(blocks // per_step,), in_specs=[pl.BlockSpec...  11.8 us
  transfers between devices with their start and end apart: 2, of which 1 were waited for; matrix products, arithmetic and copies ran while one was open for 5% of the time, Pallas kernels for 8%

profile of v3, /device:TPU:11, one launch (start us, length us, event | category | flops | bytes accessed | tf_op | source)
XLA Modules:
  0.0 438.5 jit_solution(16678433469941235281)
XLA Ops:
  0.0 0.7 broadcast_multiply_fusion
  0.7 0.1 broadcast_in_dim.21.bound_ref
  0.7 5.9 %shard_map.82 = f32[16,8,8192]{2,1,0:T(8,128)S(1)} custom-call(s32[8,128]{1,0:T(8,128)S(1)} %broadcast_in_dim.21.bound_ref, f32[4,2,8,65536]{3,2,1,0:T(8,128)} %start_high.1, f32[4,2,8,65536]{3,2,1,0:T(8,128)} %velocity_high.1), custom_call_target="tpu_custom_call" | custom-call | flops 3145728 | bytes 12582912 | tf_op jit(solution)/shard_map/pallas_call | solution.py:63
  6.6 2.0 copy-done.2
  8.6 6.7 %all-to-all-start = ((f32[16,8,8192]{2,1,0:T(8,128)}), f32[16,8,8192]{2,1,0:T(8,128)}, u32[]{:S(2)}, u32[]{:S(2)}) async-start(f32[16,8,8192]{2,1,0:T(8,128)} %copy-done.2), calls=%async_computation | async-start | bytes 8388608 | tf_op jit(solution)/shard_map/all_to_all | solution.py:391
  15.3 3.9 slice.73
  19.2 3.9 slice.74
  23.2 0.1 fusion.6
  23.3 1.4 fusion.4
  24.7 2.3 collective-permute-start
  27.0 0.7 fusion.19
  27.7 0.7 add_multiply_fusion
  28.4 0.6 compare_select_fusion
  29.0 0.6 iota_multiply_fusion
  29.6 0.7 fusion.16
  30.3 0.4 fusion.5
  30.7 0.6 convert_multiply_fusion.1
  31.4 0.1 scatter.11
  31.5 0.1 scatter.14.column_ref
  31.6 5.9 %shard_map.83.sent_ref = f32[16,8,8192]{2,1,0:T(8,128)S(1)} custom-call(s32[8,128]{1,0:T(8,128)S(1)} %broadcast_in_dim.21.bound_ref, f32[4,2,8,65536]{3,2,1,0:T(8,128)} %start_high.1, f32[4,2,8,65536]{3,2,1,0:T(8,128)} %velocity_high.1), custom_call_target="tpu_custom_call" | custom-call | flops 3145728 | bytes 12582912 | tf_op jit(solution)/shard_map/pallas_call | solution.py:63
  37.5 2.0 copy-done.3
  39.5 0.1 broadcast_in_dim.24
  39.6 0.1 broadcast_in_dim.23
  39.6 0.7 subtract_subtract_fusion
  40.4 6.5 %fusion = f32[1,128,128]{2,0,1:T(1,128)S(1)} fusion(s32[128,128]{1,0:T(8,128)S(1)} %iota_subtract_fusion, f32[]{:T(128)} %fusion.16, s32[128]{0:T(128)S(1)} %copy-done.8), kind=kOutput, calls=%fused_computation.1 | convolution fusion | flops 27263488 | bytes 131588 | tf_op jit(solution)/shard_map/dot_general | solution.py:34
  46.9 1.5 multiply_add_fusion
  48.3 70.6 %collective-permute-done.halo_ref = f32[4,65536]{1,0:T(4,128)S(1)} collective-permute-done((f32[4,65536]{1,0:T(4,128)S(1)}, f32[4,65536]{1,0:T(4,128)S(1)}, u32[]{:S(2)}, u32[]{:S(2)}) %collective-permute-start) | collective-permute-done | bytes 1048608 | tf_op jit(solution)/shard_map/ppermute | solution.py:21
  118.9 0.1 broadcast_in_dim.22.bound_ref
  119.0 28.0 %shard_map.84.slope_ref = f32[4,2,8,65536]{3,2,1,0:T(8,128)} custom-call(f32[7]{0:T(128)S(1)} %mul.103.rate_ref, s32[8,128]{1,0:T(8,128)S(1)} %broadcast_in_dim.22.bound_ref, f32[8,256]{1,0:T(8,128)S(1)} %pad_maximum_fusion.1.row_ref, f32[2,8,1024]{2,1,0:T(8,128)S(1)} %pad_maximum_fusion.diagonal_ref, f32[8,1024]{1,0:T(8,128)S(1)} %scatter.14.column_ref, ...), custom_call_target="tpu_custom_call" | custom-call | flops 125829120 | bytes 67108864 | tf_op jit(solution)/shard_map/pallas_call | solution.py:178
  147.0 276.9 %shard_map.85 = (f32[16,8,8192]{2,1,0:T(8,128)S(1)}, f32[16,8,8192]{2,1,0:T(8,128)}) custom-call(f32[128,128]{1,0:T(8,128)S(1)} %get-tuple-element.51.matrix_ref, f32[128,128]{1,0:T(8,128)S(1)} %get-tuple-element.52.episode_ref, f32[16,8,8192]{2,1,0:T(8,128)} %all-to-all-done.late_ref, f32[16,8,8192]{2,1,0:T(8,128)} %copy-done.3), custom_call_target="tpu_custom_call" | custom-call | flops 805306368 | bytes 25165824 | tf_op jit(solution)/shard_map/pallas_call | solution.py:346
  423.9 7.6 %shard_map.86.slope_ref = f32[4,2,8,65536]{3,2,1,0:T(8,128)} custom-call(s32[8,128]{1,0:T(8,128)S(1)} %broadcast_in_dim.21.bound_ref, f32[4,2,8,65536]{3,2,1,0:T(8,128)} %shard_map.84.slope_ref, f32[16,8,8192]{2,1,0:T(8,128)S(1)} %get-tuple-element.49.returned_ref), custom_call_target="tpu_custom_call", output_to_operand_aliasing={{}: (1, {})} | custom-call | flops 2097152 | bytes 12582912 | tf_op jit(solution)/shard_map/pallas_call | solution.py:224
  431.5 7.1 %shard_map.87 = f32[4,2,8,65536]{3,2,1,0:T(8,128)} custom-call(s32[8,128]{1,0:T(8,128)S(1)} %broadcast_in_dim.21.bound_ref, f32[4,2,8,65536]{3,2,1,0:T(8,128)} %shard_map.86.slope_ref, f32[16,8,8192]{2,1,0:T(8,128)S(1)} %copy-done.4), custom_call_target="tpu_custom_call", output_to_operand_aliasing={{}: (1, {})} | custom-call | flops 2097152 | bytes 12582912 | tf_op jit(solution)/shard_map/pallas_call | solution.py:224
  (27 shorter events, 0.1 us)
Async XLA Ops:
  0.0 30.3 %copy-start = (f32[16]{0:T(128)S(1)}, f32[16]{0:T(128)}, u32[]{:S(2)}) copy-start(f32[16]{0:T(128)} %param.17) | copy-start | bytes 196
  6.6 2.0 copy-start.2
  8.6 14.6 %copy-start.5 = (s32[8]{0:T(128)S(1)}, s32[8]{0:T(128)}, u32[]{:S(2)}) copy-start(s32[8]{0:T(128)} %param.20) | copy-start | bytes 100
  8.6 18.4 %copy-start.7 = (f32[7]{0:T(128)S(1)}, f32[7]{0:T(128)}, u32[]{:S(2)}) copy-start(f32[7]{0:T(128)} %param.16) | copy-start | bytes 88
  8.6 18.4 %copy-start.9 = (f32[7]{0:T(128)S(1)}, f32[7]{0:T(128)}, u32[]{:S(2)}) copy-start(f32[7]{0:T(128)} %constant.125.clone) | copy-start | bytes 88
  8.6 21.0 %copy-start.8 = (s32[128]{0:T(128)S(1)}, s32[128]{0:T(128)}, u32[]{:S(2)}) copy-start(s32[128]{0:T(128)} %param.19) | copy-start | bytes 1540
  8.6 21.7 %copy-start.6 = (s32[1024]{0:T(1024)S(1)}, s32[1024]{0:T(1024)}, u32[]{:S(2)}) copy-start(s32[1024]{0:T(1024)} %param.18) | copy-start | bytes 12292
  8.6 138.3 %all-to-all-start = ((f32[16,8,8192]{2,1,0:T(8,128)}), f32[16,8,8192]{2,1,0:T(8,128)}, u32[]{:S(2)}, u32[]{:S(2)}) async-start(f32[16,8,8192]{2,1,0:T(8,128)} %copy-done.2), calls=%async_computation | async-start | bytes 8388608 | tf_op jit(solution)/shard_map/all_to_all | solution.py:391
  24.7 94.2 %collective-permute-start = (f32[4,65536]{1,0:T(4,128)S(1)}, f32[4,65536]{1,0:T(4,128)S(1)}, u32[]{:S(2)}, u32[]{:S(2)}) collective-permute-start(f32[4,65536]{1,0:T(4,128)S(1)} %fusion.4), channel_id=1, source_target_pairs={{1,0},{2,1},{3,2},{4,3},{5,4},{6,5},{7,6},{8,7},{9,8},{10,9},{11,1... | collective-permute-start | bytes 3145736 | tf_op jit(solution)/shard_map/ppermute | solution.py:21
  37.5 2.0 copy-start.3
  423.9 7.6 %copy-start.4 = (f32[16,8,8192]{2,1,0:T(8,128)S(1)}, f32[16,8,8192]{2,1,0:T(8,128)}, u32[]{:S(2)}) copy-start(f32[16,8,8192]{2,1,0:T(8,128)} %get-tuple-element.50.returned_ref) | copy-start | bytes 12582916
  431.5 7.1 %copy-start.1 = (f32[16]{0:T(128)S(1)}, f32[16]{0:T(128)}, u32[]{:S(2)}) copy-start(f32[16]{0:T(128)} %param.17) | copy-start | bytes 196

commit v4 on v3

--- a/solution.py
+++ b/solution.py
@@ -202,41 +202,40 @@
     )(rates, bound, row_rates, diagonals, columns, start, velocity, start, velocity, start, velocity, halo)
 
 
-def add_rows(slope, returned, bound_cells, pair):
-    _, _, rows, cells = slope.shape
-    blocks = returned.shape[0]
+def add_rows(slope, early, late, bound_cells):
+    comps, _, rows, cells = slope.shape
+    blocks = early.shape[0]
     width = cells // blocks
     per_step = max(1, min(blocks, 8192 // width))
 
-    def kernel(bound_ref, slope_ref, returned_ref, out_ref):
+    def kernel(bound_ref, slope_ref, early_ref, late_ref, out_ref):
         step = pl.program_id(0)
         lane = lax.broadcasted_iota(jnp.int32, (rows, width), 1)
         for part in range(per_step):
             lanes = slice(part * width, (part + 1) * width)
             limit = bound_ref[:, 0:1] - (step * per_step + part) * width
-            for comp in range(2):
-                value = returned_ref[part, :, comp * width : (comp + 1) * width]
+            for comp in range(comps):
+                source = early_ref if comp < 2 else late_ref
+                place = (comp % 2) * width
+                value = source[part, :, place : place + width]
                 out_ref[comp, :, lanes] = slope_ref[comp, :, lanes] + jnp.where(
                     lane < limit, value, 0.0
                 )
 
-    spec = pl.BlockSpec((2, None, rows, per_step * width), lambda j: (pair, 1, 0, j))
+    spec = pl.BlockSpec((comps, None, rows, per_step * width), lambda j: (0, 1, 0, j))
+    pair = pl.BlockSpec((per_step, rows, 2 * width), lambda j: (j, 0, 0))
     return pl.pallas_call(
         kernel,
         grid=(blocks // per_step,),
-        in_specs=[
-            pl.BlockSpec((rows, 128), lambda j: (0, 0)),
-            spec,
-            pl.BlockSpec((per_step, rows, 2 * width), lambda j: (j, 0, 0)),
-        ],
+        in_specs=[pl.BlockSpec((rows, 128), lambda j: (0, 0)), spec, pair, pair],
         out_specs=spec,
         out_shape=jax.ShapeDtypeStruct(slope.shape, jnp.float32),
         input_output_aliases={1: 0},
         compiler_params=pltpu.CompilerParams(vmem_limit_bytes=VMEM_LIMIT),
         cost_estimate=pl.CostEstimate(
-            flops=4 * rows * cells, bytes_accessed=24 * rows * cells, transcendentals=0
+            flops=8 * rows * cells, bytes_accessed=48 * rows * cells, transcendentals=0
         ),
-    )(bound_cells, slope, returned)
+    )(bound_cells, slope, early, late)
 
 
 def exchange_rest(matrix, episodes, came_late, sent_early, rows):
@@ -393,9 +392,9 @@
     first_index = jnp.arange(cells, dtype=jnp.int32) // P2
     lowest = start[:, 0, 0, :] + section_step * velocity[:, 0, 0, :]
     lowest = jnp.where(first_index[None, :] < upper_bounds_per_abundance[0], lowest, 0.0)
+    lowest, bound_first = lax.optimization_barrier((lowest, bound_cells))
     halo = shifted(lowest, "slab", -1)
-
-    came_late = exchanged(on_state(start, velocity, bound_cells, 1, blocks))
+    came_late = exchanged(on_state(start, velocity, bound_first, 1, blocks))
     sent_early = on_state(start, velocity, bound_cells, 0, blocks)
 
     first_row = lax.axis_index("slab") * rows
@@ -429,8 +428,7 @@
 
     came_late, sent_early, slope = lax.optimization_barrier((came_late, sent_early, slope))
     returned_late, returned_early = exchange_rest(matrix, episodes, came_late, sent_early, rows)
-    slope = add_rows(slope, returned_late, bound_cells, 1)
-    return add_rows(slope, returned_early, bound_cells, 0)
+    return add_rows(slope, returned_early, returned_late, bound_cells)
 
 
 def solution(mesh):

time: 439 us -> 449 us (1.023)
  waiting for transfers between devices: 70.6 us -> 80.1 us
    ppermute x1, waiting for transfers between devices: 70.6 us -> 80.1 us  [shifted(): lax.ppermute(value, axis, [(source, source + steps) for source in range(f...]
    pallas_call x2 -> x1, Pallas kernels: 14.6 us -> 10.3 us  [add_rows(): pl.pallas_call(kernel, grid=(blocks // per_step,), in_specs=[pl.BlockSpec...]
  transfers between devices with their start and end apart: 2 -> 2, of which waited for: 1 -> 1; matrix products, arithmetic and copies ran while one was open for 5% -> 3% of each run, Pallas kernels for 8% -> 8%
where the time goes in v4:
time: 449 us; the launch traced here: 448 us
  Pallas kernels  327 us (73%)
  waiting for transfers between devices  80.1 us (18%)
  local copies, waits for them, and re-layouts  17.1 us (4%)
  starting transfers between devices  8.96 us (2%)
  other arithmetic  8.14 us (2%)
  matrix products  6.89 us (2%)
    pallas_call x1, Pallas kernels, exchange_rest(): pl.pallas_call(kernel, in_specs=[vmem, vmem, vmem, anywhere], out_specs=[...  277 us
    ppermute x1, waiting for transfers between devices, shifted(): lax.ppermute(value, axis, [(source, source + steps) for source in range(f...  80.1 us
    pallas_call x1, Pallas kernels, partial_slope(): pl.pallas_call(kernel, grid=(steps,), in_specs=[pl.BlockSpec(memory_space...  27.7 us
    pallas_call x2, Pallas kernels, on_state(): pl.pallas_call(kernel, grid=(blocks // per_step,), in_specs=[pl.BlockSpec...  11.8 us
    pallas_call x1, Pallas kernels, add_rows(): pl.pallas_call(kernel, grid=(blocks // per_step,), in_specs=[pl.BlockSpec...  10.3 us
  transfers between devices with their start and end apart: 2, of which 1 were waited for; matrix products, arithmetic and copies ran while one was open for 3% of the time, Pallas kernels for 8%

profile of v4, /device:TPU:11, one launch (start us, length us, event | category | flops | bytes accessed | tf_op | source)
XLA Modules:
  0.0 448.1 jit_solution(14344524400102422073)
XLA Ops:
  0.0 0.7 broadcast_multiply_fusion
  0.7 0.7 fusion.6
  1.4 3.9 slice.69
  5.3 3.9 slice.70
  9.2 1.4 fusion.4
  10.7 0.1 broadcast_in_dim.21.bound_ref
  10.7 5.9 %shard_map.82 = f32[16,8,8192]{2,1,0:T(8,128)S(1)} custom-call(s32[8,128]{1,0:T(8,128)S(1)} %broadcast_in_dim.21.bound_ref, f32[4,2,8,65536]{3,2,1,0:T(8,128)} %start_high.1, f32[4,2,8,65536]{3,2,1,0:T(8,128)} %velocity_high.1), custom_call_target="tpu_custom_call" | custom-call | flops 3145728 | bytes 12582912 | tf_op jit(solution)/shard_map/pallas_call | solution.py:63
  16.6 2.0 copy-done.2
  18.6 6.7 %all-to-all-start = ((f32[16,8,8192]{2,1,0:T(8,128)}), f32[16,8,8192]{2,1,0:T(8,128)}, u32[]{:S(2)}, u32[]{:S(2)}) async-start(f32[16,8,8192]{2,1,0:T(8,128)} %copy-done.2), calls=%async_computation | async-start | bytes 8388608 | tf_op jit(solution)/shard_map/all_to_all | solution.py:390
  25.3 2.3 collective-permute-start
  27.6 0.7 fusion.19
  28.3 0.6 add_multiply_fusion
  28.9 0.6 compare_select_fusion
  29.6 0.6 iota_multiply_fusion
  30.2 0.7 fusion.16
  30.9 0.4 fusion.5
  31.3 0.6 convert_multiply_fusion.1
  32.0 0.1 scatter.11
  32.1 0.1 scatter.14.column_ref
  32.2 5.9 %shard_map.83.sent_ref = f32[16,8,8192]{2,1,0:T(8,128)S(1)} custom-call(s32[8,128]{1,0:T(8,128)S(1)} %broadcast_in_dim.21.bound_ref, f32[4,2,8,65536]{3,2,1,0:T(8,128)} %start_high.1, f32[4,2,8,65536]{3,2,1,0:T(8,128)} %velocity_high.1), custom_call_target="tpu_custom_call" | custom-call | flops 3145728 | bytes 12582912 | tf_op jit(solution)/shard_map/pallas_call | solution.py:63
  38.1 2.0 copy-done.3
  40.1 0.1 broadcast_in_dim.26
  40.1 0.1 broadcast_in_dim.25
  40.2 0.8 subtract_subtract_fusion
  41.0 6.5 %fusion = f32[1,128,128]{2,0,1:T(1,128)S(1)} fusion(s32[128,128]{1,0:T(8,128)S(1)} %iota_subtract_fusion, f32[]{:T(128)} %fusion.16, s32[128]{0:T(128)S(1)} %copy-done.9), kind=kOutput, calls=%fused_computation.1 | convolution fusion | flops 27263488 | bytes 131588 | tf_op jit(solution)/shard_map/dot_general | solution.py:34
  47.4 1.4 multiply_add_fusion
  48.8 80.1 %collective-permute-done.halo_ref = f32[4,65536]{1,0:T(4,128)S(1)} collective-permute-done((f32[4,65536]{1,0:T(4,128)S(1)}, f32[4,65536]{1,0:T(4,128)S(1)}, u32[]{:S(2)}, u32[]{:S(2)}) %collective-permute-start) | collective-permute-done | bytes 1048608 | tf_op jit(solution)/shard_map/ppermute | solution.py:21
  129.0 27.7 %shard_map.84.slope_ref = f32[4,2,8,65536]{3,2,1,0:T(8,128)} custom-call(f32[7]{0:T(128)S(1)} %mul.105.rate_ref, s32[8,128]{1,0:T(8,128)S(1)} %broadcast_in_dim.24.bound_ref, f32[8,256]{1,0:T(8,128)S(1)} %pad_maximum_fusion.1.row_ref, f32[2,8,1024]{2,1,0:T(8,128)S(1)} %pad_maximum_fusion.diagonal_ref, f32[8,1024]{1,0:T(8,128)S(1)} %scatter.14.column_ref, ...), custom_call_target="tpu_custom_call" | custom-call | flops 125829120 | bytes 67108864 | tf_op jit(solution)/shard_map/pallas_call | solution.py:178
  156.7 276.9 %shard_map.85 = (f32[16,8,8192]{2,1,0:T(8,128)S(1)}, f32[16,8,8192]{2,1,0:T(8,128)}) custom-call(f32[128,128]{1,0:T(8,128)S(1)} %get-tuple-element.55.matrix_ref, f32[128,128]{1,0:T(8,128)S(1)} %get-tuple-element.56.episode_ref, f32[16,8,8192]{2,1,0:T(8,128)} %all-to-all-done.late_ref, f32[16,8,8192]{2,1,0:T(8,128)} %copy-done.3), custom_call_target="tpu_custom_call" | custom-call | flops 805306368 | bytes 25165824 | tf_op jit(solution)/shard_map/pallas_call | solution.py:345
  433.7 2.0 copy-done.4
  435.6 2.2 copy-done.5
  437.8 10.3 %shard_map.86 = f32[4,2,8,65536]{3,2,1,0:T(8,128)} custom-call(s32[8,128]{1,0:T(8,128)S(1)} %broadcast_in_dim.21.bound_ref, f32[4,2,8,65536]{3,2,1,0:T(8,128)} %shard_map.84.slope_ref, f32[16,8,8192]{2,1,0:T(8,128)S(1)} %copy-done.5, f32[16,8,8192]{2,1,0:T(8,128)} %copy-done.4), custom_call_target="tpu_custom_call", output_to_operand_aliasing={{}: (1, {})} | custom-call | flops 4194304 | bytes 25165824 | tf_op jit(solution)/shard_map/pallas_call | solution.py:227
  (28 shorter events, 0.2 us)
Async XLA Ops:
  0.0 30.9 %copy-start = (f32[16]{0:T(128)S(1)}, f32[16]{0:T(128)}, u32[]{:S(2)}) copy-start(f32[16]{0:T(128)} %param.17) | copy-start | bytes 196
  16.6 2.0 copy-start.2
  18.6 9.0 %copy-start.8 = (f32[7]{0:T(128)S(1)}, f32[7]{0:T(128)}, u32[]{:S(2)}) copy-start(f32[7]{0:T(128)} %param.16) | copy-start | bytes 88
  18.6 9.0 %copy-start.10 = (f32[7]{0:T(128)S(1)}, f32[7]{0:T(128)}, u32[]{:S(2)}) copy-start(f32[7]{0:T(128)} %constant.125.clone) | copy-start | bytes 88
  18.6 11.6 %copy-start.9 = (s32[128]{0:T(128)S(1)}, s32[128]{0:T(128)}, u32[]{:S(2)}) copy-start(s32[128]{0:T(128)} %param.19) | copy-start | bytes 1540
  18.6 12.3 %copy-start.7 = (s32[1024]{0:T(1024)S(1)}, s32[1024]{0:T(1024)}, u32[]{:S(2)}) copy-start(s32[1024]{0:T(1024)} %param.18) | copy-start | bytes 12292
  18.6 138.1 %all-to-all-start = ((f32[16,8,8192]{2,1,0:T(8,128)}), f32[16,8,8192]{2,1,0:T(8,128)}, u32[]{:S(2)}, u32[]{:S(2)}) async-start(f32[16,8,8192]{2,1,0:T(8,128)} %copy-done.2), calls=%async_computation | async-start | bytes 8388608 | tf_op jit(solution)/shard_map/all_to_all | solution.py:390
  25.3 103.6 %collective-permute-start = (f32[4,65536]{1,0:T(4,128)S(1)}, f32[4,65536]{1,0:T(4,128)S(1)}, u32[]{:S(2)}, u32[]{:S(2)}) collective-permute-start(f32[4,65536]{1,0:T(4,128)S(1)} %fusion.4), channel_id=1, source_target_pairs={{1,0},{2,1},{3,2},{4,3},{5,4},{6,5},{7,6},{8,7},{9,8},{10,9},{11,1... | collective-permute-start | bytes 3145736 | tf_op jit(solution)/shard_map/ppermute | solution.py:21
  32.2 96.7 %copy-start.6 = (s32[8]{0:T(128)S(1)}, s32[8]{0:T(128)}, u32[]{:S(2)}) copy-start(s32[8]{0:T(128)} %param.20) | copy-start | bytes 100
  38.1 2.0 copy-start.3
  433.6 2.0 copy-start.4
  435.6 2.2 copy-start.5
  437.8 10.3 %copy-start.1 = (f32[16]{0:T(128)S(1)}, f32[16]{0:T(128)}, u32[]{:S(2)}) copy-start(f32[16]{0:T(128)} %param.17) | copy-start | bytes 196

commit v5 on v4

--- a/solution.py
+++ b/solution.py
@@ -392,9 +392,11 @@
     first_index = jnp.arange(cells, dtype=jnp.int32) // P2
     lowest = start[:, 0, 0, :] + section_step * velocity[:, 0, 0, :]
     lowest = jnp.where(first_index[None, :] < upper_bounds_per_abundance[0], lowest, 0.0)
-    lowest, bound_first = lax.optimization_barrier((lowest, bound_cells))
     halo = shifted(lowest, "slab", -1)
-    came_late = exchanged(on_state(start, velocity, bound_first, 1, blocks))
+    sent_late, halo = lax.optimization_barrier(
+        (on_state(start, velocity, bound_cells, 1, blocks), halo)
+    )
+    came_late = exchanged(sent_late)
     sent_early = on_state(start, velocity, bound_cells, 0, blocks)
 
     first_row = lax.axis_index("slab") * rows

time: 449 us -> 417 us (0.929)
  waiting for transfers between devices: 80.1 us -> 49.7 us
    ppermute x1, waiting for transfers between devices: 80.1 us -> 6.47 us  [shifted(): lax.ppermute(value, axis, [(source, source + steps) for source in range(f...]
    all_to_all x1, waiting for transfers between devices: 0.01 us -> 43.3 us  [exchanged(): lax.all_to_all(value, 'slab', split_axis=0, concat_axis=0, tiled=True)]
  transfers between devices with their start and end apart: 2 -> 2, of which waited for: 1 -> 2; matrix products, arithmetic and copies ran while one was open for 3% -> 3% of each run, Pallas kernels for 8% -> 9%
where the time goes in v5:
time: 417 us; the launch traced here: 416 us
  Pallas kernels  327 us (78%)
  waiting for transfers between devices  49.7 us (12%)
  local copies, waits for them, and re-layouts  17.1 us (4%)
  other arithmetic  7.66 us (2%)
  starting transfers between devices  7.57 us (2%)
  matrix products  6.89 us (2%)
    pallas_call x1, Pallas kernels, exchange_rest(): pl.pallas_call(kernel, in_specs=[vmem, vmem, vmem, anywhere], out_specs=[...  277 us
    all_to_all x1, waiting for transfers between devices, exchanged(): lax.all_to_all(value, 'slab', split_axis=0, concat_axis=0, tiled=True)  43.3 us
    pallas_call x1, Pallas kernels, partial_slope(): pl.pallas_call(kernel, grid=(steps,), in_specs=[pl.BlockSpec(memory_space...  27.7 us
    pallas_call x2, Pallas kernels, on_state(): pl.pallas_call(kernel, grid=(blocks // per_step,), in_specs=[pl.BlockSpec...  11.8 us
    pallas_call x1, Pallas kernels, add_rows(): pl.pallas_call(kernel, grid=(blocks // per_step,), in_specs=[pl.BlockSpec...  10.3 us
  transfers between devices with their start and end apart: 2, of which 2 were waited for; matrix products, arithmetic and copies ran while one was open for 3% of the time, Pallas kernels for 9%

profile of v5, /device:TPU:11, one launch (start us, length us, event | category | flops | bytes accessed | tf_op | source)
XLA Modules:
  0.0 416.0 jit_solution(6334858754696647301)
XLA Ops:
  0.0 0.8 fusion.6
  0.8 3.9 slice.69
  4.7 3.9 slice.70
  8.6 1.4 fusion.4
  10.1 2.6 collective-permute-start
  12.7 0.1 broadcast_in_dim.21.bound_ref
  12.8 5.9 %shard_map.82 = f32[16,8,8192]{2,1,0:T(8,128)S(1)} custom-call(s32[8,128]{1,0:T(8,128)S(1)} %broadcast_in_dim.21.bound_ref, f32[4,2,8,65536]{3,2,1,0:T(8,128)} %start_high.1, f32[4,2,8,65536]{3,2,1,0:T(8,128)} %velocity_high.1), custom_call_target="tpu_custom_call" | custom-call | flops 3145728 | bytes 12582912 | tf_op jit(solution)/shard_map/pallas_call | solution.py:63
  18.6 2.0 copy-done.2
  20.6 6.5 %collective-permute-done.halo_ref = f32[4,65536]{1,0:T(4,128)S(1)} collective-permute-done((f32[4,65536]{1,0:T(4,128)S(1)}, f32[4,65536]{1,0:T(4,128)S(1)}, u32[]{:S(2)}, u32[]{:S(2)}) %collective-permute-start) | collective-permute-done | bytes 1048608 | tf_op jit(solution)/shard_map/ppermute | solution.py:21
  27.1 5.0 %all-to-all-start = ((f32[16,8,8192]{2,1,0:T(8,128)}), f32[16,8,8192]{2,1,0:T(8,128)}, u32[]{:S(2)}, u32[]{:S(2)}) async-start(f32[16,8,8192]{2,1,0:T(8,128)} %copy-done.2), calls=%async_computation | async-start | bytes 8388608 | tf_op jit(solution)/shard_map/all_to_all | solution.py:390
  32.1 0.4 fusion.5
  32.6 0.1 scatter.11
  32.7 0.7 fusion.19
  33.4 0.6 compare_select_fusion
  34.0 0.1 scatter.14.column_ref
  34.2 5.9 %shard_map.83.sent_ref = f32[16,8,8192]{2,1,0:T(8,128)S(1)} custom-call(s32[8,128]{1,0:T(8,128)S(1)} %broadcast_in_dim.21.bound_ref, f32[4,2,8,65536]{3,2,1,0:T(8,128)} %start_high.1, f32[4,2,8,65536]{3,2,1,0:T(8,128)} %velocity_high.1), custom_call_target="tpu_custom_call" | custom-call | flops 3145728 | bytes 12582912 | tf_op jit(solution)/shard_map/pallas_call | solution.py:63
  40.1 2.0 copy-done.3
  42.1 0.7 convert_multiply_fusion.1
  42.7 0.6 add_multiply_fusion
  43.4 0.6 iota_multiply_fusion
  44.0 0.7 fusion.16
  44.8 0.1 broadcast_in_dim.25
  44.8 0.8 subtract_subtract_fusion
  45.6 6.5 %fusion = f32[1,128,128]{2,0,1:T(1,128)S(1)} fusion(s32[128,128]{1,0:T(8,128)S(1)} %iota_subtract_fusion, f32[]{:T(128)} %fusion.16, s32[128]{0:T(128)S(1)} %copy-done.9), kind=kOutput, calls=%fused_computation.1 | convolution fusion | flops 27263488 | bytes 131588 | tf_op jit(solution)/shard_map/dot_general | solution.py:34
  52.1 1.4 multiply_add_fusion
  53.5 0.1 broadcast_in_dim.24.bound_ref
  53.5 27.7 %shard_map.84.slope_ref = f32[4,2,8,65536]{3,2,1,0:T(8,128)} custom-call(f32[7]{0:T(128)S(1)} %mul.105.rate_ref, s32[8,128]{1,0:T(8,128)S(1)} %broadcast_in_dim.24.bound_ref, f32[8,256]{1,0:T(8,128)S(1)} %pad_maximum_fusion.1.row_ref, f32[2,8,1024]{2,1,0:T(8,128)S(1)} %pad_maximum_fusion.diagonal_ref, f32[8,1024]{1,0:T(8,128)S(1)} %scatter.14.column_ref, ...), custom_call_target="tpu_custom_call" | custom-call | flops 125829120 | bytes 67108864 | tf_op jit(solution)/shard_map/pallas_call | solution.py:178
  81.3 43.3 %all-to-all-done.late_ref = f32[16,8,8192]{2,1,0:T(8,128)} async-done(((f32[16,8,8192]{2,1,0:T(8,128)}), f32[16,8,8192]{2,1,0:T(8,128)}, u32[]{:S(2)}, u32[]{:S(2)}) %all-to-all-start) | async-done | bytes 4194336 | tf_op jit(solution)/shard_map/all_to_all | solution.py:390
  124.5 277.0 %shard_map.85 = (f32[16,8,8192]{2,1,0:T(8,128)S(1)}, f32[16,8,8192]{2,1,0:T(8,128)}) custom-call(f32[128,128]{1,0:T(8,128)S(1)} %get-tuple-element.55.matrix_ref, f32[128,128]{1,0:T(8,128)S(1)} %get-tuple-element.56.episode_ref, f32[16,8,8192]{2,1,0:T(8,128)} %all-to-all-done.late_ref, f32[16,8,8192]{2,1,0:T(8,128)} %copy-done.3), custom_call_target="tpu_custom_call" | custom-call | flops 805306368 | bytes 25165824 | tf_op jit(solution)/shard_map/pallas_call | solution.py:345
  401.6 2.0 copy-done.4
  403.5 2.2 copy-done.5
  405.7 10.3 %shard_map.86 = f32[4,2,8,65536]{3,2,1,0:T(8,128)} custom-call(s32[8,128]{1,0:T(8,128)S(1)} %broadcast_in_dim.21.bound_ref, f32[4,2,8,65536]{3,2,1,0:T(8,128)} %shard_map.84.slope_ref, f32[16,8,8192]{2,1,0:T(8,128)S(1)} %copy-done.5, f32[16,8,8192]{2,1,0:T(8,128)} %copy-done.4), custom_call_target="tpu_custom_call", output_to_operand_aliasing={{}: (1, {})} | custom-call | flops 4194304 | bytes 25165824 | tf_op jit(solution)/shard_map/pallas_call | solution.py:227
  (28 shorter events, 0.2 us)
Async XLA Ops:
  0.0 32.1 %copy-start = (f32[16]{0:T(128)S(1)}, f32[16]{0:T(128)}, u32[]{:S(2)}) copy-start(f32[16]{0:T(128)} %param.17) | copy-start | bytes 196
  0.0 12.7 %copy-start.6 = (s32[8]{0:T(128)S(1)}, s32[8]{0:T(128)}, u32[]{:S(2)}) copy-start(s32[8]{0:T(128)} %param.20) | copy-start | bytes 100
  10.1 17.0 %collective-permute-start = (f32[4,65536]{1,0:T(4,128)S(1)}, f32[4,65536]{1,0:T(4,128)S(1)}, u32[]{:S(2)}, u32[]{:S(2)}) collective-permute-start(f32[4,65536]{1,0:T(4,128)S(1)} %fusion.4), channel_id=1, source_target_pairs={{1,0},{2,1},{3,2},{4,3},{5,4},{6,5},{7,6},{8,7},{9,8},{10,9},{11,1... | collective-permute-start | bytes 3145736 | tf_op jit(solution)/shard_map/ppermute | solution.py:21
  18.6 2.0 copy-start.2
  20.6 11.5 %copy-start.8 = (f32[7]{0:T(128)S(1)}, f32[7]{0:T(128)}, u32[]{:S(2)}) copy-start(f32[7]{0:T(128)} %param.16) | copy-start | bytes 88
  20.6 11.5 %copy-start.10 = (f32[7]{0:T(128)S(1)}, f32[7]{0:T(128)}, u32[]{:S(2)}) copy-start(f32[7]{0:T(128)} %constant.125.clone) | copy-start | bytes 88
  20.6 11.5 %copy-start.7 = (s32[1024]{0:T(1024)S(1)}, s32[1024]{0:T(1024)}, u32[]{:S(2)}) copy-start(s32[1024]{0:T(1024)} %param.18) | copy-start | bytes 12292
  27.1 97.4 %all-to-all-start = ((f32[16,8,8192]{2,1,0:T(8,128)}), f32[16,8,8192]{2,1,0:T(8,128)}, u32[]{:S(2)}, u32[]{:S(2)}) async-start(f32[16,8,8192]{2,1,0:T(8,128)} %copy-done.2), calls=%async_computation | async-start | bytes 8388608 | tf_op jit(solution)/shard_map/all_to_all | solution.py:390
  34.2 9.9 %copy-start.9 = (s32[128]{0:T(128)S(1)}, s32[128]{0:T(128)}, u32[]{:S(2)}) copy-start(s32[128]{0:T(128)} %param.19) | copy-start | bytes 1540
  40.1 2.0 copy-start.3
  401.5 2.0 copy-start.4
  403.5 2.2 copy-start.5
  405.7 10.3 %copy-start.1 = (f32[16]{0:T(128)S(1)}, f32[16]{0:T(128)}, u32[]{:S(2)}) copy-start(f32[16]{0:T(128)} %param.17) | copy-start | bytes 196
